TPU v7x, 32 devices: a whole 2x2x4 slice. The times are simulated.
32 devices in a mesh: dp: 4 (over x, core), tensor: 8 (over z, y).
Axes of the slice: x: 2, y: 2, z: 4, core: 2. Of those that a mesh axis runs over, the one named last changes fastest.
Arguments:
- tokens: bfloat16 [2048, 8192], P('dp', 'tensor'), may hold values from -6 to 6
- first_right: bfloat16 [32, 256, 1024], P('tensor'), may hold values from -0.375 to 0.375
- first_left: bfloat16 [128, 256, 256], P('tensor'), may hold values from -0.375 to 0.375
- second_right: bfloat16 [128, 256, 256], P('tensor'), may hold values from -0.375 to 0.375
- second_left: bfloat16 [32, 1024, 256], P('tensor'), may hold values from -0.1875 to 0.1875
- cotangent: bfloat16 [2048, 8192], P('dp', 'tensor'), may hold values from -6 to 6
Outputs:
- layer_out: bfloat16 [2048, 8192], P('dp', 'tensor')
- grad_tokens: bfloat16 [2048, 8192], P('dp', 'tensor')
- grad_first_right: float32 [32, 256, 1024], P('tensor', 'dp')
- grad_first_left: float32 [128, 256, 256], P('tensor', 'dp')
- grad_second_right: float32 [128, 256, 256], P('tensor', 'dp')
- grad_second_left: float32 [32, 1024, 256], P('tensor', 'dp')
All inputs are finite; a program needn't handle non-finite values.
Results may differ from a plain program's by a relative error of at most 0.018.
Values may be sent and summed in bfloat16 or wider, within the bound.
A program may use at most 128 MiB of HBM per device.

v0:
```python
import jax
import jax.numpy as jnp
from jax import lax
from jax.sharding import PartitionSpec as P

half_root = 0.7071067811865476
inv_root_two_pi = 0.3989422804014327


def gelu_value(value):
    return 0.5 * value * (1.0 + jax.scipy.special.erf(value * half_root))


def gelu_slope(value):
    return (
        0.5 * (1.0 + jax.scipy.special.erf(value * half_root))
        + value * jnp.exp(-0.5 * value * value) * inv_root_two_pi
    )


def shards(tokens, first_right, first_left, second_right, second_left, cotangent):
    fp = jnp.float32
    bf = jnp.bfloat16
    tok_rows = tokens.shape[0]
    in_blocks = first_right.shape[0]
    block_width = first_right.shape[1]
    wide_width = first_right.shape[2]
    hid_blocks = first_left.shape[0]
    groups = lax.axis_size("tensor")
    replicas = lax.axis_size("dp")
    all_in = in_blocks * groups
    all_hid = hid_blocks * groups
    sub_width = wide_width // all_hid
    grad_scale = float(tok_rows * replicas) ** (-0.5)
    right_one = first_right.reshape(in_blocks, block_width, all_hid, sub_width)
    right_two = second_right.reshape(hid_blocks, block_width, all_in, sub_width)
    tok_parts = tokens.reshape(tok_rows, in_blocks, block_width)
    cot_parts = cotangent.reshape(tok_rows, in_blocks, block_width)
    up_inner = jnp.einsum("tkb,kbjg->jkgt", tok_parts, right_one, preferred_element_type=fp).astype(
        bf
    )
    arrived = lax.all_to_all(up_inner, "tensor", split_axis=0, concat_axis=1, tiled=True)
    mixed_piece = arrived.reshape(hid_blocks, block_width, arrived.shape[3])
    pre_piece = jnp.einsum("jbt,jbc->jct", mixed_piece, first_left, preferred_element_type=fp)
    hidden = gelu_value(pre_piece).astype(bf)
    down_inner = jnp.einsum("jbt,jbkg->kjgt", hidden, right_two, preferred_element_type=fp).astype(
        bf
    )
    mixed_down = lax.all_to_all(down_inner, "tensor", split_axis=0, concat_axis=1, tiled=True)
    mixed_down = mixed_down.reshape(in_blocks, wide_width, tok_rows)
    layer_out = jnp.einsum(
        "kwt,kwc->tkc", mixed_down, second_left, preferred_element_type=fp
    ).astype(bf)
    layer_out = layer_out.reshape(tok_rows, in_blocks * block_width)
    reduced = {}
    d_mixed_down = jnp.einsum(
        "tkc,kwc->kwt", cot_parts, second_left, preferred_element_type=fp
    ).astype(bf)
    d_mixed_down = d_mixed_down.reshape(in_blocks, all_hid, sub_width, tok_rows)
    d_down_inner = lax.all_to_all(d_mixed_down, "tensor", split_axis=1, concat_axis=0, tiled=True)
    d_hidden = jnp.einsum("kjgt,jbkg->jbt", d_down_inner, right_two, preferred_element_type=fp)
    d_pre = (d_hidden * gelu_slope(pre_piece)).astype(bf)
    d_mixed_up = jnp.einsum("jct,jbc->jbt", d_pre, first_left, preferred_element_type=fp).astype(bf)
    d_mixed_up = d_mixed_up.reshape(hid_blocks, all_in, sub_width, tok_rows)
    d_up_inner = lax.all_to_all(d_mixed_up, "tensor", split_axis=1, concat_axis=0, tiled=True)
    grad_tokens = jnp.einsum(
        "jkgt,kbjg->tkb", d_up_inner, right_one, preferred_element_type=fp
    ).astype(bf)
    grad_tokens = grad_tokens.reshape(tok_rows, in_blocks * block_width)
    result = jnp.einsum("jbt,kjgt->bjkg", hidden, d_down_inner, preferred_element_type=fp)
    term_result = jnp.einsum("tkb,jkgt->bkjg", tok_parts, d_up_inner, preferred_element_type=fp)
    summed = (
        lax.psum_scatter(
            (term_result.reshape(block_width, in_blocks, wide_width) * grad_scale).astype(
                jnp.bfloat16
            ),
            "dp",
            scatter_dimension=0,
            tiled=True,
        ).astype(jnp.float32),
        lax.psum_scatter(
            (
                jnp.einsum("jbt,jct->bjc", mixed_piece, d_pre, preferred_element_type=fp)
                * grad_scale
            ).astype(jnp.bfloat16),
            "dp",
            scatter_dimension=0,
            tiled=True,
        ).astype(jnp.float32),
        lax.psum_scatter(
            (result.reshape(block_width, hid_blocks, block_width) * grad_scale).astype(
                jnp.bfloat16
            ),
            "dp",
            scatter_dimension=0,
            tiled=True,
        ).astype(jnp.float32),
        lax.psum_scatter(
            (
                jnp.einsum("kwt,tkc->wkc", mixed_down, cot_parts, preferred_element_type=fp)
                * grad_scale
            ).astype(jnp.bfloat16),
            "dp",
            scatter_dimension=0,
            tiled=True,
        ).astype(jnp.float32),
    )
    reduced["right_one"] = summed[0]
    reduced["left_one"] = summed[1]
    reduced["right_two"] = summed[2]
    reduced["left_two"] = summed[3]
    grad_right_one = jnp.transpose(reduced["right_one"], (1, 0, 2))
    grad_left_one = jnp.transpose(reduced["left_one"], (1, 0, 2))
    grad_right_two = jnp.transpose(reduced["right_two"], (1, 0, 2))
    grad_left_two = jnp.transpose(reduced["left_two"], (1, 0, 2))
    return (layer_out, grad_tokens, grad_right_one, grad_left_one, grad_right_two, grad_left_two)


def solution(mesh):
    in_specs = (
        P("dp", "tensor"),
        P("tensor", None, None),
        P("tensor", None, None),
        P("tensor", None, None),
        P("tensor", None, None),
        P("dp", "tensor"),
    )
    out_specs = (
        P("dp", "tensor"),
        P("dp", "tensor"),
        P("tensor", "dp", None),
        P("tensor", "dp", None),
        P("tensor", "dp", None),
        P("tensor", "dp", None),
    )
    return jax.shard_map(shards, mesh=mesh, in_specs=in_specs, out_specs=out_specs, check_vma=False)
```

profile of v0, /device:TPU:2, one launch (start us, length us, event | category | flops | bytes accessed | tf_op | source)
XLA Modules:
  0.0 493.6 jit_solution(16485045119429442879)
XLA Ops:
  7.2 4.1 copy.94
  11.3 4.6 copy.113
  20.8 4.4 copy.97
  25.2 5.8 %all-to-all-start = ((bf16[128,4,8,512]{3,2,1,0:T(8,128)(2,1)}), bf16[128,4,8,512]{3,2,1,0:T(8,128)(2,1)}, u32[]{:S(2)}, u32[]{:S(2)}) async-start(bf16[128,4,8,512]{3,2,1,0:T(8,128)(2,1)} %copy.97), calls=%async_computation | async-start | bytes 8388608 | tf_op jit(solution)/shard_map/all_to_all | solution.py:42
  36.8 87.5 %all-to-all-done = bf16[128,4,8,512]{3,2,1,0:T(8,128)(2,1)} async-done(((bf16[128,4,8,512]{3,2,1,0:T(8,128)(2,1)}), bf16[128,4,8,512]{3,2,1,0:T(8,128)(2,1)}, u32[]{:S(2)}, u32[]{:S(2)}) %all-to-all-start) | async-done | bytes 4194336 | tf_op jit(solution)/shard_map/all_to_all | solution.py:42
  124.3 4.7 all-to-all-start.2
  129.0 4.0 copy.100
  133.0 4.7 copy.98
  137.7 83.8 %all-to-all-done.2 = bf16[4,128,8,512]{3,2,0,1:T(8,128)(2,1)} async-done(((bf16[4,128,8,512]{3,2,0,1:T(8,128)(2,1)}), bf16[4,128,8,512]{3,2,0,1:T(8,128)(2,1)}, u32[]{:S(2)}, u32[]{:S(2)}) %all-to-all-start.2) | async-done | bytes 4194336 | tf_op jit(solution)/shard_map/all_to_all | solution.py:60
  221.5 6.4 %copy.168 = bf16[4,8,16,8,512]{4,0,1,3,2:T(4,128)(2,1)} copy(bf16[4,8,16,8,512]{4,3,0,2,1:T(8,128)(2,1)} %bitcast.16) | data formatting | bytes 8388608 | tf_op jit(solution)/shard_map/all_to_all | solution.py:60
  227.9 6.9 %all_to_all.57 = bf16[32,16,8,512]{3,0,2,1:T(8,128)(2,1)} reshape(bf16[8,4,16,8,512]{4,1,0,3,2:T(4,128)(2,1)} %bitcast.120) | data formatting | bytes 8388608 | tf_op jit(solution)/shard_map/all_to_all | solution.py:60
  241.8 4.7 fusion.5
  250.9 4.6 all-to-all-start.3
  255.7 4.8 fusion.19
  263.8 5.5 %convert_bitcast_fusion.2 = bf16[32,16,8,512]{3,0,2,1:T(8,128)(2,1)S(1)} fusion(bf16[16,256,32,8]{1,3,2,0:T(8,128)(2,1)} %bitcast.128, f32[16,512,256]{2,1,0:T(8,128)} %copy-done.5), kind=kOutput, calls=%fused_computation.23 | convolution fusion | flops 1086324736 | bytes 14680064 | tf_op jit(solution)/shard_map/jbt,jbkg->kjgt/dot_general | solution.py:46
  269.3 4.3 copy.103
  273.7 74.2 %all-to-all-done.3 = bf16[16,32,8,512]{3,2,0,1:T(8,128)(2,1)} async-done(((bf16[16,32,8,512]{3,2,0,1:T(8,128)(2,1)}), bf16[16,32,8,512]{3,2,0,1:T(8,128)(2,1)}, u32[]{:S(2)}, u32[]{:S(2)}) %all-to-all-start.3) | async-done | bytes 4194336 | tf_op jit(solution)/shard_map/all_to_all | solution.py:65
  347.8 4.5 all-to-all-start.1
  352.4 10.6 %fusion.13 = bf16[256,16,256]{0,2,1:T(8,128)(2,1)S(1)} fusion(bf16[32,16,8,512]{3,0,2,1:T(8,128)(2,1)} %all_to_all.57, f32[16,512,256]{2,1,0:T(8,128)} %copy-done.5), kind=kOutput, calls=%fused_computation.25 | convolution fusion | flops 1086324736 | bytes 14680064 | tf_op jit(solution)/shard_map/jbt,kjgt->bjkg/dot_general | solution.py:70
  365.8 3.7 copy.112
  375.9 69.0 %all-to-all-done.1 = bf16[32,16,8,512]{3,2,1,0:T(8,128)(2,1)} async-done(((bf16[32,16,8,512]{3,2,1,0:T(8,128)(2,1)}), bf16[32,16,8,512]{3,2,1,0:T(8,128)(2,1)}, u32[]{:S(2)}, u32[]{:S(2)}) %all-to-all-start.1) | async-done | bytes 4194336 | tf_op jit(solution)/shard_map/all_to_all | solution.py:49
  458.6 3.7 bitcast_convert_fusion
  463.6 4.4 convolution_convert_fusion
  472.1 12.9 %reduce-scatter.8.cloned.1.call-done = bf16[256,4,256]{2,0,1:T(8,128)(2,1)} async-done(((bf16[1024,4,256]{2,0,1:T(8,128)(2,1)}), bf16[256,4,256]{2,0,1:T(8,128)(2,1)}) %reduce-scatter.8.cloned.1.call-update) | async-done | bytes 524304 | tf_op jit(solution)/shard_map/reduce_scatter | solution.py:98
  (56 shorter events, 55.1 us)
Async XLA Ops:
  7.2 227.6 %copy-start = (bf16[16,256,256]{2,1,0:T(8,128)(2,1)S(1)}, bf16[16,256,256]{2,1,0:T(8,128)(2,1)}, u32[]{:S(2)}) copy-start(bf16[16,256,256]{2,1,0:T(8,128)(2,1)} %param.8) | copy-start | bytes 6291460
  25.2 99.1 %all-to-all-start = ((bf16[128,4,8,512]{3,2,1,0:T(8,128)(2,1)}), bf16[128,4,8,512]{3,2,1,0:T(8,128)(2,1)}, u32[]{:S(2)}, u32[]{:S(2)}) async-start(bf16[128,4,8,512]{3,2,1,0:T(8,128)(2,1)} %copy.97), calls=%async_computation | async-start | bytes 8388608 | tf_op jit(solution)/shard_map/all_to_all | solution.py:42
  124.3 97.2 %all-to-all-start.2 = ((bf16[4,128,8,512]{3,2,0,1:T(8,128)(2,1)}), bf16[4,128,8,512]{3,2,0,1:T(8,128)(2,1)}, u32[]{:S(2)}, u32[]{:S(2)}) async-start(bf16[4,128,8,512]{3,2,0,1:T(8,128)(2,1)} %copy.107), calls=%async_computation.2 | async-start | bytes 8388608 | tf_op jit(solution)/shard_map/all_to_all | solution.py:60
  234.8 7.0 %copy-start.7 = (bf16[32,16,8,512]{3,0,2,1:T(8,128)(2,1)S(1)}, bf16[32,16,8,512]{3,0,2,1:T(8,128)(2,1)}, u32[]{:S(2)}) copy-start(bf16[32,16,8,512]{3,0,2,1:T(8,128)(2,1)} %all_to_all.57) | copy-start | bytes 12582916
  234.8 7.0 %copy-start.8 = (bf16[16,256,256]{1,2,0:T(8,128)(2,1)S(1)}, bf16[16,256,256]{1,2,0:T(8,128)(2,1)}, u32[]{:S(2)}) copy-start(bf16[16,256,256]{1,2,0:T(8,128)(2,1)} %copy.100) | copy-start | bytes 6291460
  238.5 3.2 copy-start.5
  246.4 2.0 copy-start.4
  250.9 97.0 %all-to-all-start.3 = ((bf16[16,32,8,512]{3,2,0,1:T(8,128)(2,1)}), bf16[16,32,8,512]{3,2,0,1:T(8,128)(2,1)}, u32[]{:S(2)}, u32[]{:S(2)}) async-start(bf16[16,32,8,512]{3,2,0,1:T(8,128)(2,1)} %copy.111), calls=%async_computation.3 | async-start | bytes 8388608 | tf_op jit(solution)/shard_map/all_to_all | solution.py:65
  255.5 198.2 %reduce-scatter.4.cloned.1.call-start = ((), (), s32[]{:S(2)}) async-start(), calls=%async_computation.7 | async-start | bytes 2621440 | tf_op jit(solution)/shard_map/reduce_scatter | solution.py:81
  347.8 97.1 %all-to-all-start.1 = ((bf16[32,16,8,512]{3,2,1,0:T(8,128)(2,1)}), bf16[32,16,8,512]{3,2,1,0:T(8,128)(2,1)}, u32[]{:S(2)}, u32[]{:S(2)}) async-start(bf16[32,16,8,512]{3,2,1,0:T(8,128)(2,1)} %copy.103), calls=%async_computation.1 | async-start | bytes 8388608 | tf_op jit(solution)/shard_map/all_to_all | solution.py:49
  352.4 104.1 %reduce-scatter.6.cloned.1.call-start = ((), (), s32[]{:S(2)}) async-start(), calls=%async_computation.8 | async-start | bytes 2621440 | tf_op jit(solution)/shard_map/reduce_scatter | solution.py:90
  365.5 103.9 %all-reduce.3.cloned.1.call-start = ((), (), s32[]{:S(2)}) async-start(), calls=%async_computation.10 | async-start | bytes 4194304
  369.5 2.0 copy-start.3
  375.9 109.1 %reduce-scatter.8.cloned.1.call-start = ((), (), s32[]{:S(2)}) async-start(), calls=%async_computation.9 | async-start | bytes 2621440 | tf_op jit(solution)/shard_map/reduce_scatter | solution.py:98
  444.9 4.8 copy-start.9
  447.7 2.0 copy-start.6
  449.7 2.6 copy-start.10
  452.3 6.2 %copy-start.2 = (bf16[4,256,128,8]{2,1,3,0:T(8,128)(2,1)S(1)}, bf16[4,256,128,8]{2,1,3,0:T(8,128)(2,1)}, u32[]{:S(2)}) copy-start(bf16[4,256,128,8]{2,1,3,0:T(8,128)(2,1)} %copy.113) | copy-start | bytes 6291460
  463.6 23.5 %copy-start.1 = (bf16[16,256,256]{2,1,0:T(8,128)(2,1)S(1)}, bf16[16,256,256]{2,1,0:T(8,128)(2,1)}, u32[]{:S(2)}) copy-start(bf16[16,256,256]{2,1,0:T(8,128)(2,1)} %param.8) | copy-start | bytes 6291460
Sparse Core Ops, SparseCore 0:
  263.9 31.2 reduce-scatter.3
  365.6 31.5 reduce-scatter.5
  399.5 51.4 all-reduce.2
  453.5 31.3 reduce-scatter.7
where the time goes:
time: 497 us; the launch traced here: 494 us
  waiting for transfers between devices  327 us (66%)
  local copies, waits for them, and re-layouts  75.7 us (15%)
  matrix products  48.8 us (10%)
  starting transfers between devices  20.4 us (4%)
  between operations  14.7 us (3%)
  other arithmetic  6.57 us (1%)
    all_to_all x1, waiting for transfers between devices, shards(): lax.all_to_all(up_inner, 'tensor', split_axis=0, concat_axis=1, tiled=True)  87.5 us
    all_to_all x1, waiting for transfers between devices, shards(): lax.all_to_all(d_mixed_down, 'tensor', split_axis=1, concat_axis=0, tiled...  83.8 us
    all_to_all x1, waiting for transfers between devices, shards(): lax.all_to_all(d_mixed_up, 'tensor', split_axis=1, concat_axis=0, tiled=T...  74.2 us
    all_to_all x1, waiting for transfers between devices, shards(): lax.all_to_all(down_inner, 'tensor', split_axis=0, concat_axis=1, tiled=T...  69 us
    unnamed x29, local copies, waits for them, and re-layouts  21 us
    all_to_all x2, local copies, waits for them, and re-layouts, shards(): lax.all_to_all(d_mixed_down, 'tensor', split_axis=1, concat_axis=0, tiled...  13.3 us
    reduce_scatter x1, waiting for transfers between devices, shards(): lax.psum_scatter((jnp.einsum('kwt,tkc->wkc', mixed_down, cot_parts, prefe...  12.9 us
    dot_general x1, matrix products, shards(): jnp.einsum('jbt,kjgt->bjkg', hidden, d_down_inner, preferred_element_type...  10.6 us
  transfers between devices with their start and end apart: 8, of which 5 were waited for; matrix products, arithmetic and copies ran while one was open for 16% of the time, Pallas kernels for 0%

commit v1 on v0

v1 whole, which is shorter than its diff:
```python
import jax
import jax.numpy as jnp
from jax import lax
from jax.sharding import PartitionSpec as P

half_root = 0.7071067811865476
inv_root_two_pi = 0.3989422804014327
fp = jnp.float32
bf = jnp.bfloat16


def gelu_value(value):
    return 0.5 * value * (1.0 + jax.scipy.special.erf(value * half_root))


def gelu_slope(value):
    return (
        0.5 * (1.0 + jax.scipy.special.erf(value * half_root))
        + value * jnp.exp(-0.5 * value * value) * inv_root_two_pi
    )


def dot(spec, left, right):
    return jnp.einsum(spec, left, right, preferred_element_type=fp)


def shards(tokens, first_right, first_left, second_right, second_left, cotangent):
    tok_rows = tokens.shape[0]
    in_blocks, block_width, wide_width = first_right.shape
    hid_blocks = first_left.shape[0]
    groups = lax.axis_size("tensor")
    replicas = lax.axis_size("dp")
    members = groups // 2
    half_in = in_blocks * members
    half_hid = hid_blocks * members
    half_wide = wide_width // 2
    sub_width = wide_width // (half_hid * 2)
    half_rows = half_in * sub_width
    grad_scale = float(tok_rows * replicas) ** (-0.5)
    me = lax.axis_index("tensor")
    place = lax.axis_index("dp")
    half = me // members
    other = 1 - half
    swap = [(i, (i + members) % groups) for i in range(groups)]
    teams = [list(range(members)), list(range(members, groups))]

    def to_partner(value):
        return lax.ppermute(value, "tensor", swap)

    def within(value, split, concat):
        return lax.all_to_all(
            value, "tensor", split_axis=split, concat_axis=concat, axis_index_groups=teams, tiled=True
        )

    def cut(value, which, axis):
        size = value.shape[axis] // 2
        return lax.dynamic_slice_in_dim(value, which * size, size, axis)

    def join(mine, theirs, axis):
        return jnp.where(
            half == 0,
            jnp.concatenate([mine, theirs], axis),
            jnp.concatenate([theirs, mine], axis),
        )

    def factor_of_partner(value):
        rows = value.shape[1] // replicas
        part = lax.dynamic_slice_in_dim(value, place * rows, rows, 1)
        return lax.all_gather(to_partner(part), "dp", axis=1, tiled=True)

    def scatter_sum(value):
        return lax.psum_scatter((value * grad_scale).astype(bf), "dp", scatter_dimension=0, tiled=True)

    right_mine = cut(first_right, half, 2)
    right_theirs = factor_of_partner(cut(first_right, other, 2))
    tok_theirs = to_partner(tokens)
    last_mine = cut(second_left, half, 1)
    last_theirs = factor_of_partner(cut(second_left, other, 1))
    cot_theirs = to_partner(cotangent)

    def blocks(value):
        return value.reshape(tok_rows, in_blocks, block_width)

    def split_right(value):
        return value.reshape(in_blocks, block_width, half_hid, sub_width)

    left_one = jnp.concatenate([cut(first_left, half, 1), cut(first_left, other, 1)], 1)
    right_two = jnp.concatenate([cut(second_right, half, 2), cut(second_right, other, 2)], 2)
    right_two_mine = right_two[:, :, :half_rows].reshape(hid_blocks, block_width, half_in, sub_width)
    right_two_theirs = right_two[:, :, half_rows:].reshape(
        hid_blocks, block_width, half_in, sub_width
    )

    def up(tok, right):
        inner = dot("tkb,kbjg->jkgt", blocks(tok), split_right(right)).astype(bf)
        return within(inner, 0, 1).reshape(hid_blocks, half_rows, tok_rows)

    def up_cot(cot, last):
        last = last.reshape(in_blocks, half_hid, sub_width, block_width)
        inner = dot("tkc,kjgc->jkgt", blocks(cot), last).astype(bf)
        return within(inner, 0, 1).reshape(hid_blocks, half_rows, tok_rows)

    up_mine = up(tokens, right_mine)
    cot_mine = up_cot(cotangent, last_mine)
    up_theirs = up(tok_theirs, right_theirs)
    mixed_up = jnp.concatenate([up_mine, up_theirs], 1)
    pre_piece = dot("jbt,jbc->jct", mixed_up, left_one)
    hidden = gelu_value(pre_piece).astype(bf)

    def down(right):
        inner = dot("jbt,jbkg->kjgt", hidden, right).astype(bf)
        return within(inner, 0, 1).reshape(in_blocks, half_wide, tok_rows)

    down_theirs = down(right_two_theirs)
    down_mine = down(right_two_mine)

    d_down = jnp.concatenate([cot_mine, up_cot(cot_theirs, last_theirs)], 1)
    d_hidden = dot("jrt,jbr->jbt", d_down, right_two)
    d_pre = (d_hidden * gelu_slope(pre_piece)).astype(bf)

    def back(left):
        inner = dot("jct,jkgc->kjgt", d_pre, left.reshape(hid_blocks, half_in, sub_width, block_width))
        return within(inner.astype(bf), 0, 1).reshape(in_blocks, half_wide, tok_rows)

    d_up_theirs = back(left_one[:, half_rows:])
    d_up_mine = back(left_one[:, :half_rows])

    def together(mine, theirs):
        theirs = to_partner(theirs.astype(bf).reshape(tok_rows, in_blocks * block_width))
        return (mine.reshape(theirs.shape) + theirs.astype(fp)).astype(bf)

    layer_out = together(
        dot("kwt,kwc->tkc", down_mine, last_mine), dot("kwt,kwc->tkc", down_theirs, last_theirs)
    )
    grad_tokens = together(
        dot("kwt,kbw->tkb", d_up_mine, right_mine), dot("kwt,kbw->tkb", d_up_theirs, right_theirs)
    )

    two = dot("jbt,jrt->bjr", hidden, d_down)
    grad_right_two = scatter_sum(join(two[:, :, :half_rows], two[:, :, half_rows:], 2))
    one = dot("jrt,jct->rjc", mixed_up, d_pre)
    grad_left_one = scatter_sum(join(one[:half_rows], one[half_rows:], 0))

    last = scatter_sum(
        join(
            dot("kwt,tkc->wkc", down_mine, blocks(cotangent)),
            dot("kwt,tkc->wkc", down_theirs, blocks(cot_theirs)),
            0,
        )
    )
    near = replicas // 2
    pairs = []
    for d in range(replicas):
        for m in range(groups):
            if d // near != m // members:
                source = d * groups + m
                pairs.append((source, ((d + near) % replicas) * groups + (m + members) % groups))
    came = lax.ppermute(last, ("dp", "tensor"), pairs)
    grad_left_two = jnp.where(place // near == half, last, came)

    right_sum_theirs = to_partner(
        scatter_sum(dot("tkb,kwt->bkw", blocks(tok_theirs), d_up_theirs))
    )
    right_sum_mine = scatter_sum(dot("tkb,kwt->bkw", blocks(tokens), d_up_mine))
    grad_right_one = join(right_sum_mine, right_sum_theirs, 2)

    def last_form(value):
        return jnp.transpose(value.astype(fp), (1, 0, 2))

    return (
        layer_out,
        grad_tokens,
        last_form(grad_right_one),
        last_form(grad_left_one),
        last_form(grad_right_two),
        last_form(grad_left_two),
    )


def solution(mesh):
    in_specs = (
        P("dp", "tensor"),
        P("tensor", None, None),
        P("tensor", None, None),
        P("tensor", None, None),
        P("tensor", None, None),
        P("dp", "tensor"),
    )
    out_specs = (
        P("dp", "tensor"),
        P("dp", "tensor"),
        P("tensor", "dp", None),
        P("tensor", "dp", None),
        P("tensor", "dp", None),
        P("tensor", "dp", None),
    )
    return jax.shard_map(shards, mesh=mesh, in_specs=in_specs, out_specs=out_specs, check_vma=False)
```

time: 497 us -> 547 us (1.10)
  starting transfers between devices: 20.4 us -> 55.1 us
  waiting for transfers between devices: 327 us -> 314 us
  local copies, waits for them, and re-layouts: 75.7 us -> 88.6 us
  other arithmetic: 6.57 us -> 18.1 us
  matrix products: 48.8 us -> 54.5 us
    all_to_all x4 -> x8, waiting for transfers between devices: 315 us -> 91.4 us  [within(): lax.all_to_all(value, 'tensor', split_axis=split, concat_axis=concat, axi...]
    ppermute x0 -> x8, waiting for transfers between devices: none -> 188 us  [the longest x7 177 us: to_partner(): return lax.ppermute(value, 'tensor', swap)]
    all_gather x0 -> x2, waiting for transfers between devices: none -> 28.4 us  [factor_of_partner(): return lax.all_gather(to_partner(part), 'dp', axis=1, tiled=True)]
    ppermute x0 -> x8, starting transfers between devices: none -> 18.7 us  [the longest x7 16.7 us: to_partner(): return lax.ppermute(value, 'tensor', swap)]
    all_to_all x4 -> x8, starting transfers between devices: 19.7 us -> 35.9 us  [within(): lax.all_to_all(value, 'tensor', split_axis=split, concat_axis=concat, axi...]
    convert_element_type x0 -> x5, other arithmetic: none -> 12.4 us  [the longest x3 6.61 us: scatter_sum(): (value * grad_scale).astype(bf)]
    dynamic_slice x0 -> x8, local copies, waits for them, and re-layouts: none -> 12.4 us  [the longest x6 11.2 us: cut(): return lax.dynamic_slice_in_dim(value, which * size, size, axis)]
    reduce_scatter x3, waiting for transfers between devices: 12.9 us -> 6.05 us  [scatter_sum(): lax.psum_scatter((value * grad_scale).astype(bf), 'dp', scatter_dimension...]
  transfers between devices with their start and end apart: 8 -> 22, of which waited for: 5 -> 16; matrix products, arithmetic and copies ran while one was open for 16% -> 24% of each run, Pallas kernels for 0% -> 0%
where the time goes in v1:
time: 547 us; the launch traced here: 545 us
  waiting for transfers between devices  314 us (57%)
  local copies, waits for them, and re-layouts  88.6 us (16%)
  starting transfers between devices  55.1 us (10%)
  matrix products  54.5 us (10%)
  other arithmetic  18.1 us (3%)
  between operations  15.3 us (3%)
    ppermute x7, waiting for transfers between devices, to_partner(): return lax.ppermute(value, 'tensor', swap)  177 us
    all_to_all x8, waiting for transfers between devices, within(): lax.all_to_all(value, 'tensor', split_axis=split, concat_axis=concat, axi...  91.4 us
    dot_general x20, matrix products, dot(): return jnp.einsum(spec, left, right, preferred_element_type=fp)  54.5 us
    all_to_all x8, starting transfers between devices, within(): lax.all_to_all(value, 'tensor', split_axis=split, concat_axis=concat, axi...  35.9 us
    all_gather x2, waiting for transfers between devices, factor_of_partner(): return lax.all_gather(to_partner(part), 'dp', axis=1, tiled=True)  28.4 us
    unnamed x73, local copies, waits for them, and re-layouts  20.2 us
    all_to_all x8, local copies, waits for them, and re-layouts, within(): lax.all_to_all(value, 'tensor', split_axis=split, concat_axis=concat, axi...  20.1 us
    ppermute x7, starting transfers between devices, to_partner(): return lax.ppermute(value, 'tensor', swap)  16.7 us
  transfers between devices with their start and end apart: 22, of which 16 were waited for; matrix products, arithmetic and copies ran while one was open for 24% of the time, Pallas kernels for 0%

profile of v1, /device:TPU:2, one launch (start us, length us, event | category | flops | bytes accessed | tf_op | source)
XLA Modules:
  0.0 545.1 jit_solution(10624399064094572132)
XLA Ops:
  16.5 4.6 all-to-all-start
  26.2 20.1 %all-to-all-done = bf16[64,4,8,512]{3,2,1,0:T(8,128)(2,1)} async-done(((bf16[64,4,8,512]{3,2,1,0:T(8,128)(2,1)}), bf16[64,4,8,512]{3,2,1,0:T(8,128)(2,1)}, u32[]{:S(2)}, u32[]{:S(2)}) %all-to-all-start) | async-done | bytes 2097184 | tf_op jit(solution)/shard_map/all_to_all | solution.py:51
  54.3 24.3 %collective-permute-done.2 = bf16[4,128,256]{1,2,0:T(8,128)(2,1)S(1)} collective-permute-done((bf16[4,128,256]{1,2,0:T(8,128)(2,1)}, bf16[4,128,256]{1,2,0:T(8,128)(2,1)S(1)}, u32[]{:S(2)}, u32[]{:S(2)}) %collective-permute-start.2) | collective-permute-done | bytes 262176 | tf_op jit(solution)/shard_map/ppermute | solution.py:48
  83.9 13.5 %all-gather.5.cloned.1.call-done = bf16[4,512,256]{1,2,0:T(8,128)(2,1)} async-done(((bf16[4,128,256]{1,2,0:T(8,128)(2,1)}), bf16[4,512,256]{1,2,0:T(8,128)(2,1)}) %all-gather.5.cloned.1.call-update) | async-done | bytes 1048592 | tf_op jit(solution)/shard_map/all_gather | solution.py:69
  99.7 28.7 %collective-permute-done.4 = bf16[512,1024]{0,1:T(8,128)(2,1)S(1)} collective-permute-done((bf16[512,1024]{0,1:T(8,128)(2,1)}, bf16[512,1024]{0,1:T(8,128)(2,1)S(1)}, u32[]{:S(2)}, u32[]{:S(2)}) %collective-permute-start.4) | collective-permute-done | bytes 1048608 | tf_op jit(solution)/shard_map/ppermute | solution.py:48
  132.4 4.6 all-to-all-start.5
  140.0 23.9 %collective-permute-done = bf16[4,64,512]{2,1,0:T(8,128)(2,1)S(1)} collective-permute-done((bf16[4,64,512]{2,1,0:T(8,128)(2,1)S(1)}, bf16[4,64,512]{2,1,0:T(8,128)(2,1)S(1)}, u32[]{:S(2)}, u32[]{:S(2)}) %collective-permute-start) | collective-permute-done | bytes 262176 | tf_op jit(solution)/shard_map/ppermute | solution.py:48
  169.3 14.9 %all-gather.3.cloned.1.call-done = bf16[4,256,512]{2,1,0:T(8,128)(2,1)} async-done(((bf16[4,64,512]{2,1,0:T(8,128)(2,1)}), bf16[4,256,512]{2,1,0:T(8,128)(2,1)}) %all-gather.3.cloned.1.call-update) | async-done | bytes 1048592 | tf_op jit(solution)/shard_map/all_gather | solution.py:69
  185.8 29.0 %collective-permute-done.1 = bf16[512,1024]{0,1:T(8,128)(2,1)} collective-permute-done((bf16[512,1024]{0,1:T(8,128)(2,1)}, bf16[512,1024]{0,1:T(8,128)(2,1)}, u32[]{:S(2)}, u32[]{:S(2)}) %collective-permute-start.1) | collective-permute-done | bytes 1048608 | tf_op jit(solution)/shard_map/ppermute | solution.py:48
  241.7 5.1 all-to-all-done.1
  254.0 4.5 fusion.5
  270.9 20.7 %all-to-all-done.7 = bf16[16,16,8,512]{3,2,1,0:T(8,128)(2,1)} async-done(((bf16[16,16,8,512]{3,2,1,0:T(8,128)(2,1)}), bf16[16,16,8,512]{3,2,1,0:T(8,128)(2,1)}, u32[]{:S(2)}, u32[]{:S(2)}) %all-to-all-start.7) | async-done | bytes 2097184 | tf_op jit(solution)/shard_map/all_to_all | solution.py:51
  291.6 4.6 all-to-all-start.6
  302.3 18.3 %all-to-all-done.6 = bf16[16,16,8,512]{3,2,1,0:T(8,128)(2,1)} async-done(((bf16[16,16,8,512]{3,2,1,0:T(8,128)(2,1)}), bf16[16,16,8,512]{3,2,1,0:T(8,128)(2,1)}, u32[]{:S(2)}, u32[]{:S(2)}) %all-to-all-start.6) | async-done | bytes 2097184 | tf_op jit(solution)/shard_map/all_to_all | solution.py:51
  320.5 4.4 all-to-all-start.3
  331.1 18.7 %all-to-all-done.3 = bf16[16,16,8,512]{3,2,1,0:T(8,128)(2,1)} async-done(((bf16[16,16,8,512]{3,2,1,0:T(8,128)(2,1)}), bf16[16,16,8,512]{3,2,1,0:T(8,128)(2,1)}, u32[]{:S(2)}, u32[]{:S(2)}) %all-to-all-start.3) | async-done | bytes 2097184 | tf_op jit(solution)/shard_map/all_to_all | solution.py:51
  349.9 4.4 all-to-all-start.2
  370.2 8.5 %all-to-all-done.2 = bf16[16,16,8,512]{3,2,1,0:T(8,128)(2,1)} async-done(((bf16[16,16,8,512]{3,2,1,0:T(8,128)(2,1)}), bf16[16,16,8,512]{3,2,1,0:T(8,128)(2,1)}, u32[]{:S(2)}, u32[]{:S(2)}) %all-to-all-start.2) | async-done | bytes 2097184 | tf_op jit(solution)/shard_map/all_to_all | solution.py:51
  385.5 4.8 fusion.23
  393.4 4.7 fusion.24
  434.3 51.6 %collective-permute-done.5 = bf16[512,1024]{1,0:T(8,128)(2,1)} collective-permute-done((bf16[512,1024]{1,0:T(8,128)(2,1)}, bf16[512,1024]{1,0:T(8,128)(2,1)}, u32[]{:S(2)}, u32[]{:S(2)}) %collective-permute-start.5) | collective-permute-done | bytes 1048608 | tf_op jit(solution)/shard_map/ppermute | solution.py:48
  489.1 19.3 %collective-permute-done.3 = bf16[512,1024]{1,0:T(8,128)(2,1)} collective-permute-done((bf16[512,1024]{1,0:T(8,128)(2,1)}, bf16[512,1024]{1,0:T(8,128)(2,1)}, u32[]{:S(2)}, u32[]{:S(2)}) %collective-permute-start.3) | collective-permute-done | bytes 1048608 | tf_op jit(solution)/shard_map/ppermute | solution.py:48
  516.3 6.0 %reduce-scatter.6.cloned.1.call-done = bf16[64,16,256]{2,0,1:T(8,128)(2,1)} async-done(((bf16[256,16,256]{2,0,1:T(8,128)(2,1)}), bf16[64,16,256]{2,0,1:T(8,128)(2,1)}) %reduce-scatter.6.cloned.1.call-update) | async-done | bytes 524304 | tf_op jit(solution)/shard_map/reduce_scatter | solution.py:72
  526.4 10.9 %collective-permute-done.7 = bf16[256,4,256]{2,0,1:T(8,128)(2,1)S(1)} collective-permute-done((bf16[256,4,256]{2,0,1:T(8,128)(2,1)}, bf16[256,4,256]{2,0,1:T(8,128)(2,1)S(1)}, u32[]{:S(2)}, u32[]{:S(2)}) %collective-permute-start.7) | collective-permute-done | bytes 524320 | tf_op jit(solution)/shard_map/ppermute | solution.py:158
  (164 shorter events, 179.7 us)
Async XLA Ops:
  16.5 29.8 %all-to-all-start = ((bf16[64,4,8,512]{3,2,1,0:T(8,128)(2,1)}), bf16[64,4,8,512]{3,2,1,0:T(8,128)(2,1)}, u32[]{:S(2)}, u32[]{:S(2)}) async-start(bf16[64,4,8,512]{3,2,1,0:T(8,128)(2,1)} %copy.81), calls=%async_computation | async-start | bytes 4194304 | tf_op jit(solution)/shard_map/all_to_all | solution.py:51
  46.3 86.1 %all-to-all-start.4 = ((bf16[64,4,8,512]{3,2,1,0:T(8,128)(2,1)}), bf16[64,4,8,512]{3,2,1,0:T(8,128)(2,1)}, u32[]{:S(2)}, u32[]{:S(2)}) async-start(bf16[64,4,8,512]{3,2,1,0:T(8,128)(2,1)} %copy.99), calls=%async_computation.4 | async-start | bytes 4194304 | tf_op jit(solution)/shard_map/all_to_all | solution.py:51
  50.7 46.7 %all-gather.5.cloned.1.call-start = ((), (), s32[]{:S(2)}) async-start(), calls=%async_computation.12 | async-start | bytes 1310720 | tf_op jit(solution)/shard_map/all_gather | solution.py:69
  51.7 26.9 %collective-permute-start.2 = (bf16[4,128,256]{1,2,0:T(8,128)(2,1)}, bf16[4,128,256]{1,2,0:T(8,128)(2,1)S(1)}, u32[]{:S(2)}, u32[]{:S(2)}) collective-permute-start(bf16[4,128,256]{1,2,0:T(8,128)(2,1)} %copy.141), channel_id=1, source_target_pairs={{0,4},{1,5},{2,6},{3,7},{4,0},{5,1},{6,2},{7,3},{8,12},{9,13},{10,... | collective-permute-start | bytes 786440 | tf_op jit(solution)/shard_map/ppermute | solution.py:48
  80.7 47.7 %collective-permute-start.4 = (bf16[512,1024]{0,1:T(8,128)(2,1)}, bf16[512,1024]{0,1:T(8,128)(2,1)S(1)}, u32[]{:S(2)}, u32[]{:S(2)}) collective-permute-start(bf16[512,1024]{0,1:T(8,128)(2,1)} %copy.102), channel_id=1, source_target_pairs={{0,4},{1,5},{2,6},{3,7},{4,0},{5,1},{6,2},{7,3},{8,12},{9,13},{10,... | collective-permute-start | bytes 3145736 | tf_op jit(solution)/shard_map/ppermute | solution.py:48
  132.3 32.3 %copy-start.16 = (bf16[512,1024]{1,0:T(8,128)(2,1)S(1)}, bf16[512,1024]{1,0:T(8,128)(2,1)}, u32[]{:S(2)}) copy-start(bf16[512,1024]{1,0:T(8,128)(2,1)} %param.6) | copy-start | bytes 3145732
  132.4 86.0 %all-to-all-start.5 = ((bf16[64,4,8,512]{3,2,1,0:T(8,128)(2,1)}), bf16[64,4,8,512]{3,2,1,0:T(8,128)(2,1)}, u32[]{:S(2)}, u32[]{:S(2)}) async-start(bf16[64,4,8,512]{3,2,1,0:T(8,128)(2,1)} %copy.104), calls=%async_computation.5 | async-start | bytes 4194304 | tf_op jit(solution)/shard_map/all_to_all | solution.py:51
  136.9 47.3 %all-gather.3.cloned.1.call-start = ((), (), s32[]{:S(2)}) async-start(), calls=%async_computation.11 | async-start | bytes 1310720 | tf_op jit(solution)/shard_map/all_gather | solution.py:69
  138.1 25.7 %collective-permute-start = (bf16[4,64,512]{2,1,0:T(8,128)(2,1)S(1)}, bf16[4,64,512]{2,1,0:T(8,128)(2,1)S(1)}, u32[]{:S(2)}, u32[]{:S(2)}) collective-permute-start(bf16[4,64,512]{2,1,0:T(8,128)(2,1)S(1)} %constant_dynamic-slice_fusion.2), channel_id=1, source_target_pairs={{0,4},{1,5},{2,6},{3,7},{4,0},{5,1},{6,2},{7,3},{8,12},{9,13},{10,... | collective-permute-start | bytes 786440 | tf_op jit(solution)/shard_map/ppermute | solution.py:48
  165.9 48.8 %collective-permute-start.1 = (bf16[512,1024]{0,1:T(8,128)(2,1)}, bf16[512,1024]{0,1:T(8,128)(2,1)}, u32[]{:S(2)}, u32[]{:S(2)}) collective-permute-start(bf16[512,1024]{0,1:T(8,128)(2,1)} %copy.84), channel_id=1, source_target_pairs={{0,4},{1,5},{2,6},{3,7},{4,0},{5,1},{6,2},{7,3},{8,12},{9,13},{10,... | collective-permute-start | bytes 3145736 | tf_op jit(solution)/shard_map/ppermute | solution.py:48
  218.3 28.4 %all-to-all-start.1 = ((bf16[64,4,8,512]{3,2,1,0:T(8,128)(2,1)}), bf16[64,4,8,512]{3,2,1,0:T(8,128)(2,1)}, u32[]{:S(2)}, u32[]{:S(2)}) async-start(bf16[64,4,8,512]{3,2,1,0:T(8,128)(2,1)} %copy.86), calls=%async_computation.1 | async-start | bytes 4194304 | tf_op jit(solution)/shard_map/all_to_all | solution.py:51
  262.0 29.6 %all-to-all-start.7 = ((bf16[16,16,8,512]{3,2,1,0:T(8,128)(2,1)}), bf16[16,16,8,512]{3,2,1,0:T(8,128)(2,1)}, u32[]{:S(2)}, u32[]{:S(2)}) async-start(bf16[16,16,8,512]{3,2,1,0:T(8,128)(2,1)} %copy.109), calls=%async_computation.7 | async-start | bytes 4194304 | tf_op jit(solution)/shard_map/all_to_all | solution.py:51
  291.6 29.0 %all-to-all-start.6 = ((bf16[16,16,8,512]{3,2,1,0:T(8,128)(2,1)}), bf16[16,16,8,512]{3,2,1,0:T(8,128)(2,1)}, u32[]{:S(2)}, u32[]{:S(2)}) async-start(bf16[16,16,8,512]{3,2,1,0:T(8,128)(2,1)} %copy.106), calls=%async_computation.6 | async-start | bytes 4194304 | tf_op jit(solution)/shard_map/all_to_all | solution.py:51
  320.5 29.3 %all-to-all-start.3 = ((bf16[16,16,8,512]{3,2,1,0:T(8,128)(2,1)}), bf16[16,16,8,512]{3,2,1,0:T(8,128)(2,1)}, u32[]{:S(2)}, u32[]{:S(2)}) async-start(bf16[16,16,8,512]{3,2,1,0:T(8,128)(2,1)} %copy.92), calls=%async_computation.3 | async-start | bytes 4194304 | tf_op jit(solution)/shard_map/all_to_all | solution.py:51
  349.9 28.8 %all-to-all-start.2 = ((bf16[16,16,8,512]{3,2,1,0:T(8,128)(2,1)}), bf16[16,16,8,512]{3,2,1,0:T(8,128)(2,1)}, u32[]{:S(2)}, u32[]{:S(2)}) async-start(bf16[16,16,8,512]{3,2,1,0:T(8,128)(2,1)} %copy.88), calls=%async_computation.2 | async-start | bytes 4194304 | tf_op jit(solution)/shard_map/all_to_all | solution.py:51
  354.3 76.2 %all-reduce.5.cloned.1.call-start = ((), (), s32[]{:S(2)}) async-start(), calls=%async_computation.16 | async-start | bytes 4194304
  367.1 143.9 %reduce-scatter.8.cloned.1.call-start = ((), (), s32[]{:S(2)}) async-start(), calls=%async_computation.15 | async-start | bytes 2621440 | tf_op jit(solution)/shard_map/reduce_scatter | solution.py:72
  385.5 127.6 %reduce-scatter.4.cloned.1.call-start = ((), (), s32[]{:S(2)}) async-start(), calls=%async_computation.13 | async-start | bytes 2621440 | tf_op jit(solution)/shard_map/reduce_scatter | solution.py:72
  393.2 129.1 %reduce-scatter.6.cloned.1.call-start = ((), (), s32[]{:S(2)}) async-start(), calls=%async_computation.14 | async-start | bytes 2621440 | tf_op jit(solution)/shard_map/reduce_scatter | solution.py:72
  408.5 77.4 %collective-permute-start.5 = (bf16[512,1024]{1,0:T(8,128)(2,1)}, bf16[512,1024]{1,0:T(8,128)(2,1)}, u32[]{:S(2)}, u32[]{:S(2)}) collective-permute-start(bf16[512,1024]{1,0:T(8,128)(2,1)} %copy.111), channel_id=1, source_target_pairs={{0,4},{1,5},{2,6},{3,7},{4,0},{5,1},{6,2},{7,3},{8,12},{9,13},{10,... | collective-permute-start | bytes 3145736 | tf_op jit(solution)/shard_map/ppermute | solution.py:48
  417.0 91.3 %collective-permute-start.3 = (bf16[512,1024]{1,0:T(8,128)(2,1)}, bf16[512,1024]{1,0:T(8,128)(2,1)}, u32[]{:S(2)}, u32[]{:S(2)}) collective-permute-start(bf16[512,1024]{1,0:T(8,128)(2,1)} %copy.94), channel_id=1, source_target_pairs={{0,4},{1,5},{2,6},{3,7},{4,0},{5,1},{6,2},{7,3},{8,12},{9,13},{10,... | collective-permute-start | bytes 3145736 | tf_op jit(solution)/shard_map/ppermute | solution.py:48
  431.6 76.8 %copy-start.11 = (f32[512,1024]{1,0:T(8,128)S(1)}, f32[512,1024]{1,0:T(8,128)}, u32[]{:S(2)}) copy-start(f32[512,1024]{1,0:T(8,128)} %copy.95) | copy-start | bytes 6291460
  431.7 92.8 %collective-permute-start.6 = (bf16[64,4,512]{2,1,0:T(4,128)(2,1)S(1)}, bf16[64,4,512]{2,1,0:T(4,128)(2,1)S(1)}, u32[]{:S(2)}, u32[]{:S(2)}) collective-permute-start(bf16[64,4,512]{2,1,0:T(4,128)(2,1)S(1)} %constant_dynamic-slice_fusion.7), channel_id=1, source_target_pairs={{0,4},{1,5},{2,6},{3,7},{4,0},{5,1},{6,2},{7,3},{8,12},{9,13},{10,... | collective-permute-start | bytes 786440 | tf_op jit(solution)/shard_map/ppermute | solution.py:48
  511.0 26.2 %collective-permute-start.7 = (bf16[256,4,256]{2,0,1:T(8,128)(2,1)}, bf16[256,4,256]{2,0,1:T(8,128)(2,1)S(1)}, u32[]{:S(2)}, u32[]{:S(2)}) collective-permute-start(bf16[256,4,256]{2,0,1:T(8,128)(2,1)} %reduce-scatter.8.cloned.1.call-done), channel_id=1, source_target_pairs={{4,16},{5,17},{6,18},{7,19},{12,24},{13,25},{14,26},{15,27},{16,4}... | collective-permute-start | bytes 1572872 | tf_op jit(solution)/shard_map/ppermute | solution.py:158
  (30 other events, 146.7 us)
Sparse Core Ops, SparseCore 0:
  79.5 17.9 all-gather.4
  164.7 19.4 all-gather.2
  367.2 51.5 all-reduce.4
  421.4 31.4 reduce-scatter.7
  455.2 31.4 reduce-scatter.3
  489.2 33.0 reduce-scatter.5

commit v2 on v1

--- a/solution.py
+++ b/solution.py
@@ -22,6 +22,10 @@
 
 def dot(spec, left, right):
     return jnp.einsum(spec, left, right, preferred_element_type=fp)
+
+
+def after(value, *others):
+    return lax.optimization_barrier((value, *others))[0]
 
 
 def shards(tokens, first_right, first_left, second_right, second_left, cotangent):
@@ -68,15 +72,21 @@
         part = lax.dynamic_slice_in_dim(value, place * rows, rows, 1)
         return lax.all_gather(to_partner(part), "dp", axis=1, tiled=True)
 
+    def scaled(value):
+        return (value * grad_scale).astype(bf)
+
+    def scatter(value):
+        return lax.psum_scatter(value, "dp", scatter_dimension=0, tiled=True)
+
     def scatter_sum(value):
-        return lax.psum_scatter((value * grad_scale).astype(bf), "dp", scatter_dimension=0, tiled=True)
+        return scatter(scaled(value))
 
     right_mine = cut(first_right, half, 2)
     right_theirs = factor_of_partner(cut(first_right, other, 2))
     tok_theirs = to_partner(tokens)
     last_mine = cut(second_left, half, 1)
     last_theirs = factor_of_partner(cut(second_left, other, 1))
-    cot_theirs = to_partner(cotangent)
+    cot_theirs = to_partner(after(cotangent, tok_theirs))
 
     def blocks(value):
         return value.reshape(tok_rows, in_blocks, block_width)
@@ -91,55 +101,62 @@
         hid_blocks, block_width, half_in, sub_width
     )
 
-    def up(tok, right):
+    def up(tok, right, *first):
         inner = dot("tkb,kbjg->jkgt", blocks(tok), split_right(right)).astype(bf)
+        inner = after(inner, *first)
         return within(inner, 0, 1).reshape(hid_blocks, half_rows, tok_rows)
 
-    def up_cot(cot, last):
+    def up_cot(cot, last, *first):
         last = last.reshape(in_blocks, half_hid, sub_width, block_width)
         inner = dot("tkc,kjgc->jkgt", blocks(cot), last).astype(bf)
+        inner = after(inner, *first)
         return within(inner, 0, 1).reshape(hid_blocks, half_rows, tok_rows)
 
     up_mine = up(tokens, right_mine)
-    cot_mine = up_cot(cotangent, last_mine)
-    up_theirs = up(tok_theirs, right_theirs)
+    cot_mine = up_cot(cotangent, last_mine, up_mine)
+    up_theirs = up(tok_theirs, right_theirs, cot_mine)
+    d_down_theirs = up_cot(cot_theirs, last_theirs, up_theirs)
     mixed_up = jnp.concatenate([up_mine, up_theirs], 1)
     pre_piece = dot("jbt,jbc->jct", mixed_up, left_one)
     hidden = gelu_value(pre_piece).astype(bf)
 
-    def down(right):
+    def down(right, *first):
         inner = dot("jbt,jbkg->kjgt", hidden, right).astype(bf)
+        inner = after(inner, *first)
         return within(inner, 0, 1).reshape(in_blocks, half_wide, tok_rows)
 
-    down_theirs = down(right_two_theirs)
-    down_mine = down(right_two_mine)
-
-    d_down = jnp.concatenate([cot_mine, up_cot(cot_theirs, last_theirs)], 1)
+    def back(left, *first):
+        inner = dot("jct,jkgc->kjgt", d_pre, left.reshape(hid_blocks, half_in, sub_width, block_width))
+        inner = after(inner.astype(bf), *first)
+        return within(inner, 0, 1).reshape(in_blocks, half_wide, tok_rows)
+
+    def cross(theirs):
+        return to_partner(theirs.astype(bf).reshape(tok_rows, in_blocks * block_width))
+
+    def together(mine, came):
+        return (mine.reshape(came.shape) + came.astype(fp)).astype(bf)
+
+    down_theirs = down(right_two_theirs, d_down_theirs)
+    layer_came = cross(dot("kwt,kwc->tkc", down_theirs, last_theirs))
+
+    d_down = jnp.concatenate([cot_mine, d_down_theirs], 1)
     d_hidden = dot("jrt,jbr->jbt", d_down, right_two)
     d_pre = (d_hidden * gelu_slope(pre_piece)).astype(bf)
 
-    def back(left):
-        inner = dot("jct,jkgc->kjgt", d_pre, left.reshape(hid_blocks, half_in, sub_width, block_width))
-        return within(inner.astype(bf), 0, 1).reshape(in_blocks, half_wide, tok_rows)
-
-    d_up_theirs = back(left_one[:, half_rows:])
-    d_up_mine = back(left_one[:, :half_rows])
-
-    def together(mine, theirs):
-        theirs = to_partner(theirs.astype(bf).reshape(tok_rows, in_blocks * block_width))
-        return (mine.reshape(theirs.shape) + theirs.astype(fp)).astype(bf)
-
-    layer_out = together(
-        dot("kwt,kwc->tkc", down_mine, last_mine), dot("kwt,kwc->tkc", down_theirs, last_theirs)
-    )
-    grad_tokens = together(
-        dot("kwt,kbw->tkb", d_up_mine, right_mine), dot("kwt,kbw->tkb", d_up_theirs, right_theirs)
-    )
-
     two = dot("jbt,jrt->bjr", hidden, d_down)
-    grad_right_two = scatter_sum(join(two[:, :, :half_rows], two[:, :, half_rows:], 2))
+    two = scaled(join(two[:, :, :half_rows], two[:, :, half_rows:], 2))
     one = dot("jrt,jct->rjc", mixed_up, d_pre)
-    grad_left_one = scatter_sum(join(one[:half_rows], one[half_rows:], 0))
+    one = scaled(join(one[:half_rows], one[half_rows:], 0))
+
+    d_up_theirs = back(left_one[:, half_rows:], down_theirs, one, two)
+    grad_left_one = scatter(one)
+    grad_right_two = scatter(two)
+    grad_came = cross(dot("kwt,kbw->tkb", d_up_theirs, right_theirs))
+    down_mine = down(right_two_mine, d_up_theirs, layer_came)
+    d_up_mine = back(left_one[:, :half_rows], down_mine, grad_came, grad_left_one)
+
+    layer_out = together(dot("kwt,kwc->tkc", down_mine, last_mine), layer_came)
+    grad_tokens = together(dot("kwt,kbw->tkb", d_up_mine, right_mine), grad_came)
 
     last = scatter_sum(
         join(

time: 547 us -> 585 us (1.069)
  local copies, waits for them, and re-layouts: 88.6 us -> 102 us
  matrix products: 54.5 us -> 65.9 us
  waiting for transfers between devices: 314 us -> 322 us
    ppermute x7, waiting for transfers between devices: 177 us -> 126 us  [to_partner(): return lax.ppermute(value, 'tensor', swap)]
    unnamed x7, waiting for transfers between devices: 0.1 us -> 24.8 us
    reduce_scatter x3, waiting for transfers between devices: 6.05 us -> 30.3 us  [scatter(): return lax.psum_scatter(value, 'dp', scatter_dimension=0, tiled=True)]
    optimization_barrier x0 -> x9, local copies, waits for them, and re-layouts: none -> 15.9 us  [after(): return lax.optimization_barrier((value, *others))[0]]
    convert_element_type x10 -> x2, local copies, waits for them, and re-layouts: 16.2 us -> 4.52 us  [scaled(): return (value * grad_scale).astype(bf)]
    dot_general x20, matrix products: 54.5 us -> 65.9 us  [dot(): return jnp.einsum(spec, left, right, preferred_element_type=fp)]
    ppermute x1, waiting for transfers between devices: 10.9 us -> 17.2 us  [shards(): came = lax.ppermute(last, ('dp', 'tensor'), pairs)]
    unnamed x73 -> x70, local copies, waits for them, and re-layouts: 20.2 us -> 20.4 us
  transfers between devices with their start and end apart: 22 -> 22, of which waited for: 16 -> 16; matrix products, arithmetic and copies ran while one was open for 24% -> 25% of each run, Pallas kernels for 0% -> 0%
where the time goes in v2:
time: 585 us; the launch traced here: 583 us
  waiting for transfers between devices  322 us (55%)
  local copies, waits for them, and re-layouts  102 us (17%)
  matrix products  65.9 us (11%)
  starting transfers between devices  56.5 us (10%)
  other arithmetic  20.9 us (4%)
  between operations  15.2 us (3%)
    ppermute x7, waiting for transfers between devices, to_partner(): return lax.ppermute(value, 'tensor', swap)  126 us
    all_to_all x8, waiting for transfers between devices, within(): lax.all_to_all(value, 'tensor', split_axis=split, concat_axis=concat, axi...  95.7 us
    dot_general x20, matrix products, dot(): return jnp.einsum(spec, left, right, preferred_element_type=fp)  65.9 us
    all_to_all x8, starting transfers between devices, within(): lax.all_to_all(value, 'tensor', split_axis=split, concat_axis=concat, axi...  36 us
    reduce_scatter x3, waiting for transfers between devices, scatter(): return lax.psum_scatter(value, 'dp', scatter_dimension=0, tiled=True)  30.3 us
    all_gather x2, waiting for transfers between devices, factor_of_partner(): return lax.all_gather(to_partner(part), 'dp', axis=1, tiled=True)  27.6 us
    all_to_all x8, local copies, waits for them, and re-layouts, within(): lax.all_to_all(value, 'tensor', split_axis=split, concat_axis=concat, axi...  24.9 us
    unnamed x7, waiting for transfers between devices  24.8 us
  transfers between devices with their start and end apart: 22, of which 16 were waited for; matrix products, arithmetic and copies ran while one was open for 25% of the time, Pallas kernels for 0%

profile of v2, /device:TPU:2, one launch (start us, length us, event | category | flops | bytes accessed | tf_op | source)
XLA Modules:
  0.0 582.9 jit_solution(17172358797589996561)
XLA Ops:
  16.5 4.6 all-to-all-start
  26.0 20.3 %all-to-all-done = bf16[64,4,8,512]{3,2,1,0:T(8,128)(2,1)} async-done(((bf16[64,4,8,512]{3,2,1,0:T(8,128)(2,1)}), bf16[64,4,8,512]{3,2,1,0:T(8,128)(2,1)}, u32[]{:S(2)}, u32[]{:S(2)}) %all-to-all-start) | async-done | bytes 2097184 | tf_op jit(solution)/shard_map/all_to_all | solution.py:55
  59.7 23.9 %collective-permute-done = bf16[4,64,512]{2,1,0:T(8,128)(2,1)S(1)} collective-permute-done((bf16[4,64,512]{2,1,0:T(8,128)(2,1)S(1)}, bf16[4,64,512]{2,1,0:T(8,128)(2,1)S(1)}, u32[]{:S(2)}, u32[]{:S(2)}) %collective-permute-start) | collective-permute-done | bytes 262176 | tf_op jit(solution)/shard_map/ppermute | solution.py:52
  89.9 12.4 %all-gather.3.cloned.1.call-done = bf16[4,256,512]{2,1,0:T(8,128)(2,1)} async-done(((bf16[4,64,512]{2,1,0:T(8,128)(2,1)}), bf16[4,256,512]{2,1,0:T(8,128)(2,1)}) %all-gather.3.cloned.1.call-update) | async-done | bytes 1048592 | tf_op jit(solution)/shard_map/all_gather | solution.py:73
  104.6 29.8 %collective-permute-done.1 = bf16[512,1024]{0,1:T(8,128)(2,1)} collective-permute-done((bf16[512,1024]{0,1:T(8,128)(2,1)}, bf16[512,1024]{0,1:T(8,128)(2,1)}, u32[]{:S(2)}, u32[]{:S(2)}) %collective-permute-start.1) | collective-permute-done | bytes 1048608 | tf_op jit(solution)/shard_map/ppermute | solution.py:52
  150.1 24.2 %collective-permute-done.2 = bf16[4,128,256]{1,2,0:T(8,128)(2,1)S(1)} collective-permute-done((bf16[4,128,256]{1,2,0:T(8,128)(2,1)}, bf16[4,128,256]{1,2,0:T(8,128)(2,1)S(1)}, u32[]{:S(2)}, u32[]{:S(2)}) %collective-permute-start.2) | collective-permute-done | bytes 262176 | tf_op jit(solution)/shard_map/ppermute | solution.py:52
  179.7 15.2 %all-gather.5.cloned.1.call-done = bf16[4,512,256]{1,2,0:T(8,128)(2,1)} async-done(((bf16[4,128,256]{1,2,0:T(8,128)(2,1)}), bf16[4,512,256]{1,2,0:T(8,128)(2,1)}) %all-gather.5.cloned.1.call-update) | async-done | bytes 1048592 | tf_op jit(solution)/shard_map/all_gather | solution.py:73
  197.1 27.9 %collective-permute-done.3 = bf16[512,1024]{0,1:T(8,128)(2,1)S(1)} collective-permute-done((bf16[512,1024]{0,1:T(8,128)(2,1)}, bf16[512,1024]{0,1:T(8,128)(2,1)S(1)}, u32[]{:S(2)}, u32[]{:S(2)}) %collective-permute-start.3) | collective-permute-done | bytes 1048608 | tf_op jit(solution)/shard_map/ppermute | solution.py:52
  233.8 4.5 all-to-all-start.3
  249.9 6.2 %multiply_convert_fusion = (bf16[16,256,512]{2,1,0:T(8,128)(2,1)S(1)}, f32[16,256,512]{2,1,0:T(8,128)}) fusion(bf16[16,128,512]{2,1,0:T(8,128)(2,1)} %bitcast.186, bf16[16,128,512]{2,1,0:T(8,128)(2,1)} %bitcast.182, bf16[16,128,256]{1,2,0:T(8,128)(2,1)} %copy.142, bf16[16,128,256]{1,2,0:T(8,128)(2,1)} %copy.141), kind=kOutput, calls=%fused_computation.7 | convolution fusion | flops 1096810496 | bytes 18874368 | tf_op jit(solution)/shard_map/jbt,jbc->jct/dot_general | solution.py:24
  267.3 4.6 all-to-all-start.4
  272.0 7.2 %fusion.5 = bf16[16,256,512]{2,1,0:T(8,128)(2,1)S(1)} fusion(f32[16,256,512]{2,1,0:T(8,128)} %get-tuple-element.51, bf16[16,128,512]{2,1,0:T(8,128)(2,1)} %bitcast.188, bf16[16,128,512]{2,1,0:T(8,128)(2,1)} %bitcast.184, bf16[16,256,128]{2,1,0:T(8,128)(2,1)} %get-tuple-element.46, bf16[16,256,128]{2,1,0:T(8,128)(2,1)} %get-tuple-element.47), kind=kOutput, calls=%fused_computation.6 | convolution fusion | flops 1107296256 | bytes 18874368 | tf_op jit(solution)/shard_map/jrt,jbr->jbt/dot_general | solution.py:24
  291.8 5.4 fusion.9
  297.2 4.6 convert_bitcast_fusion.2
  320.6 5.1 convert_bitcast_fusion.4
  325.7 26.0 %all-to-all-done.5 = bf16[16,16,8,512]{3,2,1,0:T(8,128)(2,1)} async-done(((bf16[16,16,8,512]{3,2,1,0:T(8,128)(2,1)}), bf16[16,16,8,512]{3,2,1,0:T(8,128)(2,1)}, u32[]{:S(2)}, u32[]{:S(2)}) %all-to-all-start.5) | async-done | bytes 2097184 | tf_op jit(solution)/shard_map/all_to_all | solution.py:55
  355.0 10.6 %collective-permute-done.4 = bf16[512,1024]{1,0:T(8,128)(2,1)} collective-permute-done((bf16[512,1024]{1,0:T(8,128)(2,1)}, bf16[512,1024]{1,0:T(8,128)(2,1)}, u32[]{:S(2)}, u32[]{:S(2)}) %collective-permute-start.4) | collective-permute-done | bytes 1048608 | tf_op jit(solution)/shard_map/ppermute | solution.py:52
  382.2 29.3 %all-to-all-done.6 = bf16[16,16,8,512]{3,2,1,0:T(8,128)(2,1)} async-done(((bf16[16,16,8,512]{3,2,1,0:T(8,128)(2,1)}), bf16[16,16,8,512]{3,2,1,0:T(8,128)(2,1)}, u32[]{:S(2)}, u32[]{:S(2)}) %all-to-all-start.6) | async-done | bytes 2097184 | tf_op jit(solution)/shard_map/all_to_all | solution.py:55
  414.6 9.9 %collective-permute-done.5 = bf16[512,1024]{1,0:T(8,128)(2,1)} collective-permute-done((bf16[512,1024]{1,0:T(8,128)(2,1)}, bf16[512,1024]{1,0:T(8,128)(2,1)}, u32[]{:S(2)}, u32[]{:S(2)}) %collective-permute-start.5) | collective-permute-done | bytes 1048608 | tf_op jit(solution)/shard_map/ppermute | solution.py:52
  436.8 17.9 %all-to-all-done.7 = bf16[16,16,8,512]{3,2,1,0:T(8,128)(2,1)} async-done(((bf16[16,16,8,512]{3,2,1,0:T(8,128)(2,1)}), bf16[16,16,8,512]{3,2,1,0:T(8,128)(2,1)}, u32[]{:S(2)}, u32[]{:S(2)}) %all-to-all-start.7) | async-done | bytes 2097184 | tf_op jit(solution)/shard_map/all_to_all | solution.py:55
  488.0 24.1 %all-reduce.5.cloned.1.call-done = (bf16[256,4,512]{2,1,0:T(4,128)(2,1)}, bf16[256,4,512]{2,1,0:T(4,128)(2,1)}) async-done(((bf16[256,4,512]{2,1,0:T(4,128)(2,1)}, bf16[256,4,512]{2,1,0:T(4,128)(2,1)}), (bf16[256,4,512]{2,1,0:T(4,128)(2,1)}, bf16[256,4,512]{2,1,0:T(4,128)(2,1)})) %all-reduce.5.cloned.1.call-update) | async-done | bytes 2097168
  515.8 30.3 %reduce-scatter.8.cloned.1.call-done = bf16[256,4,256]{2,0,1:T(8,128)(2,1)} async-done(((bf16[1024,4,256]{2,0,1:T(8,128)(2,1)}), bf16[256,4,256]{2,0,1:T(8,128)(2,1)}) %reduce-scatter.8.cloned.1.call-update) | async-done | bytes 524304 | tf_op jit(solution)/shard_map/reduce_scatter | solution.py:79
  546.0 5.4 collective-permute-start.7
  557.8 17.2 %collective-permute-done.7 = bf16[256,4,256]{2,0,1:T(8,128)(2,1)S(1)} collective-permute-done((bf16[256,4,256]{2,0,1:T(8,128)(2,1)}, bf16[256,4,256]{2,0,1:T(8,128)(2,1)S(1)}, u32[]{:S(2)}, u32[]{:S(2)}) %collective-permute-start.7) | collective-permute-done | bytes 524320 | tf_op jit(solution)/shard_map/ppermute | solution.py:175
  (162 shorter events, 200.9 us)
Async XLA Ops:
  7.2 15.6 %copy-start = (bf16[4,1024,256]{2,1,0:T(8,128)(2,1)S(1)}, bf16[4,1024,256]{2,1,0:T(8,128)(2,1)}, u32[]{:S(2)}) copy-start(bf16[4,1024,256]{2,1,0:T(8,128)(2,1)} %param.10) | copy-start | bytes 6291460
  16.5 29.8 %all-to-all-start = ((bf16[64,4,8,512]{3,2,1,0:T(8,128)(2,1)}), bf16[64,4,8,512]{3,2,1,0:T(8,128)(2,1)}, u32[]{:S(2)}, u32[]{:S(2)}) async-start(bf16[64,4,8,512]{3,2,1,0:T(8,128)(2,1)} %copy.83), calls=%async_computation | async-start | bytes 4194304 | tf_op jit(solution)/shard_map/all_to_all | solution.py:55
  51.3 86.8 %all-to-all-start.1 = ((bf16[64,4,8,512]{3,2,1,0:T(8,128)(2,1)}), bf16[64,4,8,512]{3,2,1,0:T(8,128)(2,1)}, u32[]{:S(2)}, u32[]{:S(2)}) async-start(bf16[64,4,8,512]{3,2,1,0:T(8,128)(2,1)} %copy.90), calls=%async_computation.1 | async-start | bytes 4194304 | tf_op jit(solution)/shard_map/all_to_all | solution.py:55
  55.8 46.6 %all-gather.3.cloned.1.call-start = ((), (), s32[]{:S(2)}) async-start(), calls=%async_computation.11 | async-start | bytes 1310720 | tf_op jit(solution)/shard_map/all_gather | solution.py:73
  57.0 26.5 %collective-permute-start = (bf16[4,64,512]{2,1,0:T(8,128)(2,1)S(1)}, bf16[4,64,512]{2,1,0:T(8,128)(2,1)S(1)}, u32[]{:S(2)}, u32[]{:S(2)}) collective-permute-start(bf16[4,64,512]{2,1,0:T(8,128)(2,1)S(1)} %constant_dynamic-slice_fusion.2), channel_id=1, source_target_pairs={{0,4},{1,5},{2,6},{3,7},{4,0},{5,1},{6,2},{7,3},{8,12},{9,13},{10,... | collective-permute-start | bytes 786440 | tf_op jit(solution)/shard_map/ppermute | solution.py:52
  86.5 47.9 %collective-permute-start.1 = (bf16[512,1024]{0,1:T(8,128)(2,1)}, bf16[512,1024]{0,1:T(8,128)(2,1)}, u32[]{:S(2)}, u32[]{:S(2)}) collective-permute-start(bf16[512,1024]{0,1:T(8,128)(2,1)} %copy.86), channel_id=1, source_target_pairs={{0,4},{1,5},{2,6},{3,7},{4,0},{5,1},{6,2},{7,3},{8,12},{9,13},{10,... | collective-permute-start | bytes 3145736 | tf_op jit(solution)/shard_map/ppermute | solution.py:52
  143.0 85.8 %all-to-all-start.2 = ((bf16[64,4,8,512]{3,2,1,0:T(8,128)(2,1)}), bf16[64,4,8,512]{3,2,1,0:T(8,128)(2,1)}, u32[]{:S(2)}, u32[]{:S(2)}) async-start(bf16[64,4,8,512]{3,2,1,0:T(8,128)(2,1)} %copy.92), calls=%async_computation.2 | async-start | bytes 4194304 | tf_op jit(solution)/shard_map/all_to_all | solution.py:55
  147.4 47.4 %all-gather.5.cloned.1.call-start = ((), (), s32[]{:S(2)}) async-start(), calls=%async_computation.12 | async-start | bytes 1310720 | tf_op jit(solution)/shard_map/all_gather | solution.py:73
  148.4 25.9 %collective-permute-start.2 = (bf16[4,128,256]{1,2,0:T(8,128)(2,1)}, bf16[4,128,256]{1,2,0:T(8,128)(2,1)S(1)}, u32[]{:S(2)}, u32[]{:S(2)}) collective-permute-start(bf16[4,128,256]{1,2,0:T(8,128)(2,1)} %copy.143), channel_id=1, source_target_pairs={{0,4},{1,5},{2,6},{3,7},{4,0},{5,1},{6,2},{7,3},{8,12},{9,13},{10,... | collective-permute-start | bytes 786440 | tf_op jit(solution)/shard_map/ppermute | solution.py:52
  176.4 48.7 %collective-permute-start.3 = (bf16[512,1024]{0,1:T(8,128)(2,1)}, bf16[512,1024]{0,1:T(8,128)(2,1)S(1)}, u32[]{:S(2)}, u32[]{:S(2)}) collective-permute-start(bf16[512,1024]{0,1:T(8,128)(2,1)} %copy.97), channel_id=1, source_target_pairs={{0,4},{1,5},{2,6},{3,7},{4,0},{5,1},{6,2},{7,3},{8,12},{9,13},{10,... | collective-permute-start | bytes 3145736 | tf_op jit(solution)/shard_map/ppermute | solution.py:52
  233.8 28.6 %all-to-all-start.3 = ((bf16[64,4,8,512]{3,2,1,0:T(8,128)(2,1)}), bf16[64,4,8,512]{3,2,1,0:T(8,128)(2,1)}, u32[]{:S(2)}, u32[]{:S(2)}) async-start(bf16[64,4,8,512]{3,2,1,0:T(8,128)(2,1)} %copy.99), calls=%async_computation.3 | async-start | bytes 4194304 | tf_op jit(solution)/shard_map/all_to_all | solution.py:55
  267.3 34.5 %all-to-all-start.4 = ((bf16[16,16,8,512]{3,2,1,0:T(8,128)(2,1)}), bf16[16,16,8,512]{3,2,1,0:T(8,128)(2,1)}, u32[]{:S(2)}, u32[]{:S(2)}) async-start(bf16[16,16,8,512]{3,2,1,0:T(8,128)(2,1)} %copy.102), calls=%async_computation.4 | async-start | bytes 4194304 | tf_op jit(solution)/shard_map/all_to_all | solution.py:55
  306.7 44.9 %all-to-all-start.5 = ((bf16[16,16,8,512]{3,2,1,0:T(8,128)(2,1)}), bf16[16,16,8,512]{3,2,1,0:T(8,128)(2,1)}, u32[]{:S(2)}, u32[]{:S(2)}) async-start(bf16[16,16,8,512]{3,2,1,0:T(8,128)(2,1)} %copy.105), calls=%async_computation.5 | async-start | bytes 4194304 | tf_op jit(solution)/shard_map/all_to_all | solution.py:55
  311.2 103.4 %reduce-scatter.4.cloned.1.call-start = ((), (), s32[]{:S(2)}) async-start(), calls=%async_computation.13 | async-start | bytes 2621440 | tf_op jit(solution)/shard_map/reduce_scatter | solution.py:79
  317.8 47.8 %collective-permute-start.4 = (bf16[512,1024]{1,0:T(8,128)(2,1)}, bf16[512,1024]{1,0:T(8,128)(2,1)}, u32[]{:S(2)}, u32[]{:S(2)}) collective-permute-start(bf16[512,1024]{1,0:T(8,128)(2,1)} %copy.107), channel_id=1, source_target_pairs={{0,4},{1,5},{2,6},{3,7},{4,0},{5,1},{6,2},{7,3},{8,12},{9,13},{10,... | collective-permute-start | bytes 3145736 | tf_op jit(solution)/shard_map/ppermute | solution.py:52
  367.2 44.3 %all-to-all-start.6 = ((bf16[16,16,8,512]{3,2,1,0:T(8,128)(2,1)}), bf16[16,16,8,512]{3,2,1,0:T(8,128)(2,1)}, u32[]{:S(2)}, u32[]{:S(2)}) async-start(bf16[16,16,8,512]{3,2,1,0:T(8,128)(2,1)} %copy.108), calls=%async_computation.6 | async-start | bytes 4194304 | tf_op jit(solution)/shard_map/all_to_all | solution.py:55
  371.7 99.2 %reduce-scatter.6.cloned.1.call-start = ((), (), s32[]{:S(2)}) async-start(), calls=%async_computation.14 | async-start | bytes 2621440 | tf_op jit(solution)/shard_map/reduce_scatter | solution.py:79
  377.6 46.9 %collective-permute-start.5 = (bf16[512,1024]{1,0:T(8,128)(2,1)}, bf16[512,1024]{1,0:T(8,128)(2,1)}, u32[]{:S(2)}, u32[]{:S(2)}) collective-permute-start(bf16[512,1024]{1,0:T(8,128)(2,1)} %copy.112), channel_id=1, source_target_pairs={{0,4},{1,5},{2,6},{3,7},{4,0},{5,1},{6,2},{7,3},{8,12},{9,13},{10,... | collective-permute-start | bytes 3145736 | tf_op jit(solution)/shard_map/ppermute | solution.py:52
  427.7 27.1 %all-to-all-start.7 = ((bf16[16,16,8,512]{3,2,1,0:T(8,128)(2,1)}), bf16[16,16,8,512]{3,2,1,0:T(8,128)(2,1)}, u32[]{:S(2)}, u32[]{:S(2)}) async-start(bf16[16,16,8,512]{3,2,1,0:T(8,128)(2,1)} %copy.113), calls=%async_computation.8 | async-start | bytes 4194304 | tf_op jit(solution)/shard_map/all_to_all | solution.py:55
  432.1 79.9 %all-reduce.5.cloned.1.call-start = ((), (), s32[]{:S(2)}) async-start(), calls=%async_computation.16 | async-start | bytes 4194304
  462.4 83.6 %reduce-scatter.8.cloned.1.call-start = ((), (), s32[]{:S(2)}) async-start(), calls=%async_computation.15 | async-start | bytes 2621440 | tf_op jit(solution)/shard_map/reduce_scatter | solution.py:79
  513.1 42.7 %collective-permute-start.6 = (bf16[64,4,512]{2,1,0:T(4,128)(2,1)S(1)}, bf16[64,4,512]{2,1,0:T(4,128)(2,1)S(1)}, u32[]{:S(2)}, u32[]{:S(2)}) collective-permute-start(bf16[64,4,512]{2,1,0:T(4,128)(2,1)S(1)} %constant_dynamic-slice_fusion.7), channel_id=1, source_target_pairs={{0,4},{1,5},{2,6},{3,7},{4,0},{5,1},{6,2},{7,3},{8,12},{9,13},{10,... | collective-permute-start | bytes 786440 | tf_op jit(solution)/shard_map/ppermute | solution.py:52
  546.0 28.9 %collective-permute-start.7 = (bf16[256,4,256]{2,0,1:T(8,128)(2,1)}, bf16[256,4,256]{2,0,1:T(8,128)(2,1)S(1)}, u32[]{:S(2)}, u32[]{:S(2)}) collective-permute-start(bf16[256,4,256]{2,0,1:T(8,128)(2,1)} %reduce-scatter.8.cloned.1.call-done), channel_id=1, source_target_pairs={{4,16},{5,17},{6,18},{7,19},{12,24},{13,25},{14,26},{15,27},{16,4}... | collective-permute-start | bytes 1572872 | tf_op jit(solution)/shard_map/ppermute | solution.py:175
  554.7 20.3 %copy-start.27 = (bf16[256,4,256]{2,0,1:T(8,128)(2,1)S(1)}, bf16[256,4,256]{2,0,1:T(8,128)(2,1)}, u32[]{:S(2)}) copy-start(bf16[256,4,256]{2,0,1:T(8,128)(2,1)} %reduce-scatter.8.cloned.1.call-done) | copy-start | bytes 1572868
  (29 other events, 104.3 us)
Sparse Core Ops, SparseCore 0:
  84.4 17.8 all-gather.2
  175.2 19.6 all-gather.4
  314.6 29.8 reduce-scatter.3
  378.1 31.7 reduce-scatter.5
  462.6 49.4 all-reduce.4
  514.6 31.4 reduce-scatter.7

commit v3 on v2

v3 whole, which is shorter than its diff:
```python
import jax
import jax.numpy as jnp
from jax import lax
from jax.sharding import PartitionSpec as P

half_root = 0.7071067811865476
inv_root_two_pi = 0.3989422804014327
fp = jnp.float32
bf = jnp.bfloat16


def gelu_value(value):
    return 0.5 * value * (1.0 + jax.scipy.special.erf(value * half_root))


def gelu_slope(value):
    return (
        0.5 * (1.0 + jax.scipy.special.erf(value * half_root))
        + value * jnp.exp(-0.5 * value * value) * inv_root_two_pi
    )


def dot(spec, left, right):
    return jnp.einsum(spec, left, right, preferred_element_type=fp)


def after(value, *others):
    for item in others:
        first = lax.slice(item, (0,) * item.ndim, (1,) * item.ndim).reshape(())
        value = value + (first * jnp.zeros((), first.dtype)).astype(value.dtype)
    return value


def shards(tokens, first_right, first_left, second_right, second_left, cotangent):
    tok_rows = tokens.shape[0]
    in_blocks, block_width, wide_width = first_right.shape
    hid_blocks = first_left.shape[0]
    groups = lax.axis_size("tensor")
    replicas = lax.axis_size("dp")
    members = groups // 2
    half_in = in_blocks * members
    half_hid = hid_blocks * members
    all_in = in_blocks * groups
    sub_width = wide_width // (half_hid * 2)
    half_rows = half_in * sub_width
    grad_scale = float(tok_rows * replicas) ** (-0.5)
    me = lax.axis_index("tensor")
    place = lax.axis_index("dp")
    half = me // members
    other = 1 - half
    swap = [(i, (i + members) % groups) for i in range(groups)]
    teams = [list(range(members)), list(range(members, groups))]

    def to_partner(value):
        return lax.ppermute(value, "tensor", swap)

    def within(value, split, concat):
        return lax.all_to_all(
            value, "tensor", split_axis=split, concat_axis=concat, axis_index_groups=teams, tiled=True
        )

    def cut(value, which, axis):
        size = value.shape[axis] // 2
        return lax.dynamic_slice_in_dim(value, which * size, size, axis)

    def join(mine, theirs, axis):
        return jnp.where(
            half == 0,
            jnp.concatenate([mine, theirs], axis),
            jnp.concatenate([theirs, mine], axis),
        )

    def part_of(value):
        rows = value.shape[1] // replicas
        return lax.dynamic_slice_in_dim(value, place * rows, rows, 1)

    def scaled(value):
        return (value * grad_scale).astype(bf)

    def scatter(value):
        return lax.psum_scatter(value, "dp", scatter_dimension=0, tiled=True)

    def scatter_sum(value):
        return scatter(scaled(value))

    right_mine = cut(first_right, half, 2)
    last_mine = cut(second_left, half, 1)
    right_part = part_of(cut(first_right, other, 2))
    last_part = part_of(cut(second_left, other, 1))
    parts = to_partner(jnp.concatenate([right_part.reshape(-1, 128), last_part.reshape(-1, 128)], 0))
    tok_theirs = to_partner(after(tokens, parts))
    edge = right_part.size // 128
    right_theirs = lax.all_gather(parts[:edge].reshape(right_part.shape), "dp", axis=1, tiled=True)
    last_theirs = lax.all_gather(parts[edge:].reshape(last_part.shape), "dp", axis=1, tiled=True)

    def blocks(value):
        return value.reshape(tok_rows, in_blocks, block_width)

    def split_right(value):
        return value.reshape(in_blocks, block_width, half_hid, sub_width)

    left_one = jnp.concatenate([cut(first_left, half, 1), cut(first_left, other, 1)], 1)
    right_two = jnp.concatenate([cut(second_right, half, 2), cut(second_right, other, 2)], 2)
    right_two_whole = second_right.reshape(hid_blocks, block_width, all_in, sub_width)
    left_one_whole = first_left.reshape(hid_blocks, all_in, sub_width, block_width)

    def up(tok, right):
        return dot("tkb,kbjg->jkgt", blocks(tok), split_right(right)).astype(bf)

    def up_cot(cot, last):
        last = last.reshape(in_blocks, half_hid, sub_width, block_width)
        return dot("tkc,kjgc->jkgt", blocks(cot), last).astype(bf)

    def rows(value):
        return value.reshape(hid_blocks, half_rows, tok_rows)

    up_mine = within(after(up(tokens, right_mine), parts), 0, 1)
    cot_mine = within(after(up_cot(cotangent, last_mine), up_mine), 0, 1)
    cot_theirs = to_partner(after(cotangent, tok_theirs, up_mine))
    up_theirs = within(after(up(tok_theirs, right_theirs), cot_mine), 0, 1)
    d_down_theirs = within(after(up_cot(cot_theirs, last_theirs), up_theirs), 0, 1)
    mixed_up = jnp.concatenate([rows(up_mine), rows(up_theirs)], 1)
    pre_piece = dot("jbt,jbc->jct", mixed_up, left_one)
    hidden = gelu_value(pre_piece).astype(bf)

    def home(value, *first):
        value = after(value.astype(bf), *first)
        value = lax.all_to_all(value, "tensor", split_axis=0, concat_axis=1, tiled=True)
        return value.reshape(in_blocks, wide_width, tok_rows)

    mixed_down = home(dot("jbt,jbkg->kjgt", hidden, right_two_whole), d_down_theirs)

    d_down = jnp.concatenate([rows(cot_mine), rows(d_down_theirs)], 1)
    d_hidden = dot("jrt,jbr->jbt", d_down, right_two)
    d_pre = (d_hidden * gelu_slope(pre_piece)).astype(bf)
    back = dot("jct,jkgc->kjgt", d_pre, left_one_whole)

    two = dot("jbt,jrt->bjr", hidden, d_down)
    two = scaled(join(two[:, :, :half_rows], two[:, :, half_rows:], 2))
    one = dot("jrt,jct->rjc", mixed_up, d_pre)
    one = scaled(join(one[:half_rows], one[half_rows:], 0))

    grad_left_one = scatter(one)
    grad_right_two = scatter(two)
    d_up = home(back, mixed_down, grad_left_one, grad_right_two)
    grad_left_two = scatter(scaled(dot("kwt,tkc->wkc", mixed_down, blocks(cotangent))))
    grad_right_one = scatter(scaled(dot("tkb,kwt->bkw", blocks(tokens), d_up)))

    def merged(value):
        return value.astype(bf).reshape(tok_rows, in_blocks * block_width)

    layer_out = merged(dot("kwt,kwc->tkc", mixed_down, second_left))
    grad_tokens = merged(dot("kwt,kbw->tkb", d_up, first_right))

    def last_form(value):
        return jnp.transpose(value.astype(fp), (1, 0, 2))

    return (
        layer_out,
        grad_tokens,
        last_form(grad_right_one),
        last_form(grad_left_one),
        last_form(grad_right_two),
        last_form(grad_left_two),
    )


def solution(mesh):
    in_specs = (
        P("dp", "tensor"),
        P("tensor", None, None),
        P("tensor", None, None),
        P("tensor", None, None),
        P("tensor", None, None),
        P("dp", "tensor"),
    )
    out_specs = (
        P("dp", "tensor"),
        P("dp", "tensor"),
        P("tensor", "dp", None),
        P("tensor", "dp", None),
        P("tensor", "dp", None),
        P("tensor", "dp", None),
    )
    return jax.shard_map(shards, mesh=mesh, in_specs=in_specs, out_specs=out_specs, check_vma=False)
```

time: 585 us -> 558 us (0.954); the launches traced: 583 us -> 548 us
  starting transfers between devices: 56.5 us -> 35.7 us
  matrix products: 65.9 us -> 48.1 us
  between operations: 15.2 us -> 21.7 us
    all_to_all x0 -> x2, waiting for transfers between devices: none -> 123 us  [home(): lax.all_to_all(value, 'tensor', split_axis=0, concat_axis=1, tiled=True)]
    ppermute x7 -> x3, waiting for transfers between devices: 126 us -> 71.3 us  [to_partner(): return lax.ppermute(value, 'tensor', swap)]
    all_to_all x8 -> x4, waiting for transfers between devices: 95.7 us -> 61.9 us  [within(): lax.all_to_all(value, 'tensor', split_axis=split, concat_axis=concat, axi...]
    all_gather x2, waiting for transfers between devices: 27.6 us -> 0.04 us  [the longest x1 0.02 us: shards(): lax.all_gather(parts[:edge].reshape(right_part.shape), 'dp', axis=1, tile...]
    all_to_all x8 -> x4, starting transfers between devices: 36 us -> 17.8 us  [within(): lax.all_to_all(value, 'tensor', split_axis=split, concat_axis=concat, axi...]
    dot_general x20 -> x14, matrix products: 65.9 us -> 48.1 us  [dot(): return jnp.einsum(spec, left, right, preferred_element_type=fp)]
    all_to_all x8 -> x4, local copies, waits for them, and re-layouts: 24.9 us -> 7.55 us  [within(): lax.all_to_all(value, 'tensor', split_axis=split, concat_axis=concat, axi...]
    ppermute x1 -> x0, waiting for transfers between devices: 17.2 us -> none  [shards(): came = lax.ppermute(last, ('dp', 'tensor'), pairs)]
  transfers between devices with their start and end apart: 22 -> 15, of which waited for: 16 -> 10; matrix products, arithmetic and copies ran while one was open for 25% -> 19% of each run, Pallas kernels for 0% -> 0%
where the time goes in v3:
time: 558 us; the launch traced here: 548 us
  waiting for transfers between devices  323 us (58%)
  local copies, waits for them, and re-layouts  103 us (18%)
  matrix products  48.1 us (9%)
  starting transfers between devices  35.7 us (6%)
  between operations  21.7 us (4%)
  other arithmetic  15.5 us (3%)
    all_to_all x2, waiting for transfers between devices, home(): lax.all_to_all(value, 'tensor', split_axis=0, concat_axis=1, tiled=True)  123 us
    ppermute x3, waiting for transfers between devices, to_partner(): return lax.ppermute(value, 'tensor', swap)  71.3 us
    all_to_all x4, waiting for transfers between devices, within(): lax.all_to_all(value, 'tensor', split_axis=split, concat_axis=concat, axi...  61.9 us
    dot_general x14, matrix products, dot(): return jnp.einsum(spec, left, right, preferred_element_type=fp)  48.1 us
    unnamed x7, waiting for transfers between devices  37.2 us
    reduce_scatter x3, waiting for transfers between devices, scatter(): return lax.psum_scatter(value, 'dp', scatter_dimension=0, tiled=True)  29.8 us
    unnamed x60, local copies, waits for them, and re-layouts  26.4 us
    all_to_all x4, starting transfers between devices, within(): lax.all_to_all(value, 'tensor', split_axis=split, concat_axis=concat, axi...  17.8 us
  transfers between devices with their start and end apart: 15, of which 10 were waited for; matrix products, arithmetic and copies ran while one was open for 19% of the time, Pallas kernels for 0%

profile of v3, /device:TPU:2, one launch (start us, length us, event | category | flops | bytes accessed | tf_op | source)
XLA Modules:
  0.0 547.7 jit_solution(7732163565936873134)
XLA Ops:
  20.8 17.4 %collective-permute-done = bf16[2048,128]{1,0:T(8,128)(2,1)} collective-permute-done((bf16[2048,128]{1,0:T(8,128)(2,1)}, bf16[2048,128]{1,0:T(8,128)(2,1)}, u32[]{:S(2)}, u32[]{:S(2)}) %collective-permute-start) | collective-permute-done | bytes 524320 | tf_op jit(solution)/shard_map/ppermute | solution.py:55
  43.9 4.4 all-to-all-start
  51.0 21.7 %all-to-all-done = bf16[64,4,8,512]{3,2,1,0:T(8,128)(2,1)} async-done(((bf16[64,4,8,512]{3,2,1,0:T(8,128)(2,1)}), bf16[64,4,8,512]{3,2,1,0:T(8,128)(2,1)}, u32[]{:S(2)}, u32[]{:S(2)}) %all-to-all-start) | async-done | bytes 2097184 | tf_op jit(solution)/shard_map/all_to_all | solution.py:58
  91.2 45.4 %collective-permute-done.1 = bf16[512,1024]{1,0:T(8,128)(2,1)} collective-permute-done((bf16[512,1024]{1,0:T(8,128)(2,1)S(1)}, bf16[512,1024]{1,0:T(8,128)(2,1)}, u32[]{:S(2)}, u32[]{:S(2)}) %collective-permute-start.1) | collective-permute-done | bytes 1048608 | tf_op jit(solution)/shard_map/ppermute | solution.py:55
  146.1 4.5 all-to-all-start.2
  158.8 32.8 %all-to-all-done.2 = bf16[64,4,8,512]{3,2,1,0:T(8,128)(2,1)} async-done(((bf16[64,4,8,512]{3,2,1,0:T(8,128)(2,1)}), bf16[64,4,8,512]{3,2,1,0:T(8,128)(2,1)}, u32[]{:S(2)}, u32[]{:S(2)}) %all-to-all-start.2) | async-done | bytes 2097184 | tf_op jit(solution)/shard_map/all_to_all | solution.py:58
  196.0 8.4 %collective-permute-done.2 = bf16[512,1024]{0,1:T(8,128)(2,1)S(1)} collective-permute-done((bf16[512,1024]{0,1:T(8,128)(2,1)}, bf16[512,1024]{0,1:T(8,128)(2,1)S(1)}, u32[]{:S(2)}, u32[]{:S(2)}) %collective-permute-start.2) | collective-permute-done | bytes 1048608 | tf_op jit(solution)/shard_map/ppermute | solution.py:55
  208.1 4.5 all-to-all-start.3
  221.9 6.7 %multiply_convert_fusion = (bf16[16,256,512]{2,1,0:T(8,128)(2,1)}, f32[16,256,512]{2,1,0:T(8,128)}) fusion(bf16[16,128,512]{2,1,0:T(8,128)(2,1)S(1)} %bitcast.153, bf16[16,128,512]{2,1,0:T(8,128)(2,1)S(1)} %bitcast.147, bf16[16,128,256]{1,2,0:T(8,128)(2,1)} %copy.181, bf16[16,128,256]{1,2,0:T(8,128)(2,1)} %copy.180), kind=kOutput, calls=%fused_computation.7 | convolution fusion | flops 1096810496 | bytes 18874368 | tf_op jit(solution)/shard_map/jbt,jbc->jct/dot_general | solution.py:24
  228.6 7.3 %all-to-all-done.3 = bf16[64,4,8,512]{3,2,1,0:T(8,128)(2,1)} async-done(((bf16[64,4,8,512]{3,2,1,0:T(8,128)(2,1)}), bf16[64,4,8,512]{3,2,1,0:T(8,128)(2,1)}, u32[]{:S(2)}, u32[]{:S(2)}) %all-to-all-start.3) | async-done | bytes 2097184 | tf_op jit(solution)/shard_map/all_to_all | solution.py:58
  239.2 6.5 %fusion.5 = bf16[16,256,512]{2,1,0:T(8,128)(2,1)S(1)} fusion(f32[16,256,512]{2,1,0:T(8,128)} %get-tuple-element.47, bf16[16,128,512]{2,1,0:T(8,128)(2,1)S(1)} %bitcast.155, bf16[16,128,512]{2,1,0:T(8,128)(2,1)S(1)} %bitcast.151, bf16[16,256,128]{2,1,0:T(8,128)(2,1)S(1)} %copy-done.19, bf16[16,256,128]{2,1,0:T(8,128)(2,1)S(1)} %get-tuple-element.40), kind=kOutput, calls=%fused_computation.6 | convolution fusion | flops 1107296256 | bytes 18874368 | tf_op jit(solution)/shard_map/jrt,jbr->jbt/dot_general | solution.py:24
  250.5 4.6 fusion.7
  261.0 4.6 add_bitcast_fusion.1
  270.0 4.6 all-to-all-start.4
  274.6 6.8 %fusion.14 = f32[16,256,256]{2,1,0:T(8,128)} fusion(bf16[16,256,512]{2,1,0:T(8,128)(2,1)} %get-tuple-element.46, bf16[16,128,512]{2,1,0:T(8,128)(2,1)} %bitcast.157, bf16[16,128,512]{2,1,0:T(8,128)(2,1)} %bitcast.150), kind=kOutput, calls=%fused_computation.26 | convolution fusion | flops 1082130432 | bytes 12582912 | tf_op jit(solution)/shard_map/jbt,jrt->bjr/dot_general | solution.py:24
  281.4 5.5 %copy.154 = f32[16,256,256]{1,0,2:T(8,128)} copy(f32[16,256,256]{2,1,0:T(8,128)} %fusion.14) | data formatting | bytes 8388608 | tf_op jit(solution)/shard_map/jbt,jrt->bjr/dot_general | solution.py:24
  294.4 29.8 %reduce-scatter.6.cloned.1.call-done = bf16[64,16,256]{2,1,0:T(8,128)(2,1)} async-done(((bf16[256,16,256]{2,1,0:T(8,128)(2,1)}), bf16[64,16,256]{2,1,0:T(8,128)(2,1)}) %reduce-scatter.6.cloned.1.call-update) | async-done | bytes 524304 | tf_op jit(solution)/shard_map/reduce_scatter | solution.py:81
  325.9 41.3 %all-to-all-done.4 = bf16[32,16,8,512]{3,2,1,0:T(8,128)(2,1)} async-done(((bf16[32,16,8,512]{3,2,1,0:T(8,128)(2,1)}), bf16[32,16,8,512]{3,2,1,0:T(8,128)(2,1)}, u32[]{:S(2)}, u32[]{:S(2)}) %all-to-all-start.4) | async-done | bytes 4194336 | tf_op jit(solution)/shard_map/all_to_all | solution.py:128
  374.5 4.4 copy.155
  378.9 4.7 all-to-all-start.5
  383.7 4.8 fusion.30
  394.5 81.7 %all-to-all-done.5 = bf16[32,16,8,512]{3,2,1,0:T(8,128)(2,1)} async-done(((bf16[32,16,8,512]{3,2,1,0:T(8,128)(2,1)}), bf16[32,16,8,512]{3,2,1,0:T(8,128)(2,1)}, u32[]{:S(2)}, u32[]{:S(2)}) %all-to-all-start.5) | async-done | bytes 4194336 | tf_op jit(solution)/shard_map/all_to_all | solution.py:128
  483.6 4.5 copy.158
  500.5 37.1 %all-reduce.3.cloned.1.call-done = bf16[256,4,1024]{2,1,0:T(4,128)(2,1)} async-done(((bf16[256,4,1024]{2,1,0:T(4,128)(2,1)}), bf16[256,4,1024]{2,1,0:T(4,128)(2,1)}) %all-reduce.3.cloned.1.call-update) | async-done | bytes 2097168
  (136 shorter events, 132.0 us)
Async XLA Ops:
  7.2 12.1 %copy-start.3 = (bf16[512,1024]{1,0:T(8,128)(2,1)S(1)}, bf16[512,1024]{1,0:T(8,128)(2,1)}, u32[]{:S(2)}) copy-start(bf16[512,1024]{1,0:T(8,128)(2,1)} %param.6) | copy-start | bytes 3145732
  12.1 26.1 %collective-permute-start = (bf16[2048,128]{1,0:T(8,128)(2,1)}, bf16[2048,128]{1,0:T(8,128)(2,1)}, u32[]{:S(2)}, u32[]{:S(2)}) collective-permute-start(bf16[2048,128]{1,0:T(8,128)(2,1)} %pad_maximum_fusion.6), channel_id=1, source_target_pairs={{0,4},{1,5},{2,6},{3,7},{4,0},{5,1},{6,2},{7,3},{8,12},{9,13},{10,... | collective-permute-start | bytes 1572872 | tf_op jit(solution)/shard_map/ppermute | solution.py:55
  43.9 28.8 %all-to-all-start = ((bf16[64,4,8,512]{3,2,1,0:T(8,128)(2,1)}), bf16[64,4,8,512]{3,2,1,0:T(8,128)(2,1)}, u32[]{:S(2)}, u32[]{:S(2)}) async-start(bf16[64,4,8,512]{3,2,1,0:T(8,128)(2,1)} %copy.129), calls=%async_computation | async-start | bytes 4194304 | tf_op jit(solution)/shard_map/all_to_all | solution.py:58
  79.6 60.9 %all-to-all-start.1 = ((bf16[64,4,8,512]{3,2,1,0:T(8,128)(2,1)}), bf16[64,4,8,512]{3,2,1,0:T(8,128)(2,1)}, u32[]{:S(2)}, u32[]{:S(2)}) async-start(bf16[64,4,8,512]{3,2,1,0:T(8,128)(2,1)} %copy.136), calls=%async_computation.1 | async-start | bytes 4194304 | tf_op jit(solution)/shard_map/all_to_all | solution.py:58
  84.0 54.1 %all-gather.3.cloned.1.call-start = ((), (), s32[]{:S(2)}) async-start(), calls=%async_computation.9 | async-start | bytes 1310720 | tf_op jit(solution)/shard_map/all_gather | solution.py:93
  87.7 48.9 %collective-permute-start.1 = (bf16[512,1024]{1,0:T(8,128)(2,1)S(1)}, bf16[512,1024]{1,0:T(8,128)(2,1)}, u32[]{:S(2)}, u32[]{:S(2)}) collective-permute-start(bf16[512,1024]{1,0:T(8,128)(2,1)S(1)} %broadcast_add_fusion), channel_id=1, source_target_pairs={{0,4},{1,5},{2,6},{3,7},{4,0},{5,1},{6,2},{7,3},{8,12},{9,13},{10,... | collective-permute-start | bytes 3145736 | tf_op jit(solution)/shard_map/ppermute | solution.py:55
  144.4 7.0 %copy-start.7 = (bf16[512,1024]{1,0:T(8,128)(2,1)S(1)}, bf16[512,1024]{1,0:T(8,128)(2,1)}, u32[]{:S(2)}) copy-start(bf16[512,1024]{1,0:T(8,128)(2,1)} %param.11) | copy-start | bytes 3145732
  146.1 45.5 %all-to-all-start.2 = ((bf16[64,4,8,512]{3,2,1,0:T(8,128)(2,1)}), bf16[64,4,8,512]{3,2,1,0:T(8,128)(2,1)}, u32[]{:S(2)}, u32[]{:S(2)}) async-start(bf16[64,4,8,512]{3,2,1,0:T(8,128)(2,1)} %copy.138), calls=%async_computation.2 | async-start | bytes 4194304 | tf_op jit(solution)/shard_map/all_to_all | solution.py:58
  150.6 45.5 %all-gather.5.cloned.1.call-start = ((), (), s32[]{:S(2)}) async-start(), calls=%async_computation.10 | async-start | bytes 1310720 | tf_op jit(solution)/shard_map/all_gather | solution.py:94
  156.8 47.6 %collective-permute-start.2 = (bf16[512,1024]{0,1:T(8,128)(2,1)}, bf16[512,1024]{0,1:T(8,128)(2,1)S(1)}, u32[]{:S(2)}, u32[]{:S(2)}) collective-permute-start(bf16[512,1024]{0,1:T(8,128)(2,1)} %add_add_fusion), channel_id=1, source_target_pairs={{0,4},{1,5},{2,6},{3,7},{4,0},{5,1},{6,2},{7,3},{8,12},{9,13},{10,... | collective-permute-start | bytes 3145736 | tf_op jit(solution)/shard_map/ppermute | solution.py:55
  208.1 27.9 %all-to-all-start.3 = ((bf16[64,4,8,512]{3,2,1,0:T(8,128)(2,1)}), bf16[64,4,8,512]{3,2,1,0:T(8,128)(2,1)}, u32[]{:S(2)}, u32[]{:S(2)}) async-start(bf16[64,4,8,512]{3,2,1,0:T(8,128)(2,1)} %copy.145), calls=%async_computation.3 | async-start | bytes 4194304 | tf_op jit(solution)/shard_map/all_to_all | solution.py:58
  212.5 80.0 %reduce-scatter.4.cloned.1.call-start = ((), (), s32[]{:S(2)}) async-start(), calls=%async_computation.11 | async-start | bytes 2621440 | tf_op jit(solution)/shard_map/reduce_scatter | solution.py:81
  239.2 6.5 %copy-start.12 = (bf16[16,4,4,8,512]{4,3,2,1,0:T(8,128)(2,1)S(1)}, bf16[16,4,4,8,512]{4,3,2,1,0:T(8,128)(2,1)}, u32[]{:S(2)}) copy-start(bf16[16,4,4,8,512]{4,3,2,1,0:T(8,128)(2,1)} %copy-done.10) | copy-start | bytes 6291460
  239.2 6.5 %copy-start.17 = (bf16[16,4,4,8,512]{4,3,2,1,0:T(8,128)(2,1)S(1)}, bf16[16,4,4,8,512]{4,3,2,1,0:T(8,128)(2,1)}, u32[]{:S(2)}) copy-start(bf16[16,4,4,8,512]{4,3,2,1,0:T(8,128)(2,1)} %copy-done.15) | copy-start | bytes 6291460
  270.0 97.2 %all-to-all-start.4 = ((bf16[32,16,8,512]{3,2,1,0:T(8,128)(2,1)}), bf16[32,16,8,512]{3,2,1,0:T(8,128)(2,1)}, u32[]{:S(2)}, u32[]{:S(2)}) async-start(bf16[32,16,8,512]{3,2,1,0:T(8,128)(2,1)} %copy.147), calls=%async_computation.4 | async-start | bytes 8388608 | tf_op jit(solution)/shard_map/all_to_all | solution.py:128
  274.6 49.5 %reduce-scatter.6.cloned.1.call-start = ((), (), s32[]{:S(2)}) async-start(), calls=%async_computation.12 | async-start | bytes 2621440 | tf_op jit(solution)/shard_map/reduce_scatter | solution.py:81
  367.2 6.0 %copy-start.9 = (bf16[16,256,256]{2,1,0:T(8,128)(2,1)S(1)}, bf16[16,256,256]{2,1,0:T(8,128)(2,1)}, u32[]{:S(2)}) copy-start(bf16[16,256,256]{2,1,0:T(8,128)(2,1)} %param.8) | copy-start | bytes 6291460
  367.2 6.0 %copy-start.24 = (bf16[16,256,512]{2,1,0:T(8,128)(2,1)S(1)}, bf16[16,256,512]{2,1,0:T(8,128)(2,1)}, u32[]{:S(2)}) copy-start(bf16[16,256,512]{2,1,0:T(8,128)(2,1)} %copy-done.23) | copy-start | bytes 12582916
  378.9 4.7 copy-start.8
  378.9 97.3 %all-to-all-start.5 = ((bf16[32,16,8,512]{3,2,1,0:T(8,128)(2,1)}), bf16[32,16,8,512]{3,2,1,0:T(8,128)(2,1)}, u32[]{:S(2)}, u32[]{:S(2)}) async-start(bf16[32,16,8,512]{3,2,1,0:T(8,128)(2,1)} %copy.155), calls=%async_computation.7 | async-start | bytes 8388608 | tf_op jit(solution)/shard_map/all_to_all | solution.py:128
  383.6 109.3 %reduce-scatter.8.cloned.1.call-start = ((), (), s32[]{:S(2)}) async-start(), calls=%async_computation.13 | async-start | bytes 2621440 | tf_op jit(solution)/shard_map/reduce_scatter | solution.py:81
  383.7 5.1 copy-start.22
  388.5 149.1 %all-reduce.3.cloned.1.call-start = ((), (), s32[]{:S(2)}) async-start(), calls=%async_computation.14 | async-start | bytes 4194304
  476.2 4.7 copy-start.4
  (16 other events, 41.2 us)
Sparse Core Ops, SparseCore 0:
  87.8 17.8 all-gather.2
  153.5 16.8 all-gather.4
  255.3 29.1 reduce-scatter.3
  292.6 31.4 reduce-scatter.5
  388.6 31.4 reduce-scatter.7
  488.2 49.3 all-reduce.2

commit v4 on v0

v4 whole, which is shorter than its diff:
```python
import jax
import jax.numpy as jnp
from jax import lax
from jax.sharding import PartitionSpec as P

half_root = 0.7071067811865476
inv_root_two_pi = 0.3989422804014327


def gelu_value(value):
    return 0.5 * value * (1.0 + jax.scipy.special.erf(value * half_root))


def gelu_slope(value):
    return (
        0.5 * (1.0 + jax.scipy.special.erf(value * half_root))
        + value * jnp.exp(-0.5 * value * value) * inv_root_two_pi
    )


def shards(tokens, first_right, first_left, second_right, second_left, cotangent):
    fp = jnp.float32
    bf = jnp.bfloat16
    tok_rows = tokens.shape[0]
    in_blocks, block_width, wide_width = first_right.shape
    hid_blocks = first_left.shape[0]
    groups = lax.axis_size("tensor")
    replicas = lax.axis_size("dp")
    all_in = in_blocks * groups
    all_hid = hid_blocks * groups
    sub_width = wide_width // all_hid
    grad_scale = float(tok_rows * replicas) ** (-0.5)
    right_one = first_right.reshape(in_blocks, block_width, all_hid, sub_width)
    right_two = second_right.reshape(hid_blocks, block_width, all_in, sub_width)
    tok_parts = tokens.reshape(tok_rows, in_blocks, block_width)
    cot_parts = cotangent.reshape(tok_rows, in_blocks, block_width)

    def dot(spec, left, right):
        return jnp.einsum(spec, left, right, preferred_element_type=fp)

    def exchange(value):
        return lax.all_to_all(value, "tensor", split_axis=0, concat_axis=1, tiled=True)

    def summed(value):
        lead, rows, width = value.shape
        value = (value * grad_scale).astype(bf)
        value = value.reshape(lead, replicas, rows // replicas, width)
        value = jnp.transpose(value, (1, 0, 2, 3))
        return lax.psum_scatter(value, "dp", scatter_dimension=0, tiled=False).astype(fp)

    arrived = exchange(dot("tkb,kbjg->jkgt", tok_parts, right_one).astype(bf))
    last_four = second_left.reshape(in_blocks, all_hid, sub_width, block_width)
    d_sent = dot("tkc,kjgc->jkgt", cot_parts, last_four).astype(bf)
    d_sent, arrived = lax.optimization_barrier((d_sent, arrived))
    d_arrived = exchange(d_sent)

    mixed_piece = arrived.reshape(hid_blocks, block_width, tok_rows)
    pre_piece = dot("jbt,jbc->jct", mixed_piece, first_left)
    hidden = gelu_value(pre_piece).astype(bf)
    down_sent = dot("jbt,jbkg->kjgt", hidden, right_two).astype(bf)
    down_sent, d_arrived = lax.optimization_barrier((down_sent, d_arrived))
    mixed_down = exchange(down_sent)

    d_down = d_arrived.reshape(hid_blocks, block_width, tok_rows)
    d_hidden = dot("jrt,jbr->jbt", d_down, second_right)
    d_pre = (d_hidden * gelu_slope(pre_piece)).astype(bf)

    pieces = 2 if in_blocks % 2 == 0 else 1
    part = in_blocks // pieces
    left_parts = first_left.reshape(hid_blocks, groups, in_blocks, sub_width, block_width)

    def back(place):
        left = left_parts[:, :, place * part : (place + 1) * part]
        left = left.reshape(hid_blocks, groups * part, sub_width, block_width)
        return dot("jct,jkgc->kjgt", d_pre, left).astype(bf)

    sent = [back(place) for place in range(pieces)]
    sent[0], mixed_down = lax.optimization_barrier((sent[0], mixed_down))
    grad_left_one = summed(dot("jbt,jct->jbc", mixed_piece, d_pre))
    grad_right_two = summed(dot("jbt,jrt->jbr", hidden, d_down))
    mixed_down = mixed_down.reshape(in_blocks, wide_width, tok_rows)

    token_parts = []
    sum_parts = []
    for place in range(pieces):
        d_up = exchange(sent[place])
        if place + 1 < pieces:
            sent[place + 1], d_up, grad_left_one, grad_right_two = lax.optimization_barrier(
                (sent[place + 1], d_up, grad_left_one, grad_right_two)
            )
        d_up = d_up.reshape(part, wide_width, tok_rows)
        chosen = slice(place * part, (place + 1) * part)
        sum_parts.append(summed(dot("tkb,kwt->kbw", tok_parts[:, chosen], d_up)))
        token_parts.append(dot("kwt,kbw->tkb", d_up, first_right[chosen]).astype(bf))
    grad_left_two = summed(dot("kwt,tkc->kwc", mixed_down, cot_parts))
    layer_out = dot("kwt,kwc->tkc", mixed_down, second_left).astype(bf)
    layer_out = layer_out.reshape(tok_rows, in_blocks * block_width)
    grad_tokens = jnp.concatenate(token_parts, 1).reshape(tok_rows, in_blocks * block_width)
    grad_right_one = jnp.concatenate(sum_parts, 0)
    return (layer_out, grad_tokens, grad_right_one, grad_left_one, grad_right_two, grad_left_two)


def solution(mesh):
    in_specs = (
        P("dp", "tensor"),
        P("tensor", None, None),
        P("tensor", None, None),
        P("tensor", None, None),
        P("tensor", None, None),
        P("dp", "tensor"),
    )
    out_specs = (
        P("dp", "tensor"),
        P("dp", "tensor"),
        P("tensor", "dp", None),
        P("tensor", "dp", None),
        P("tensor", "dp", None),
        P("tensor", "dp", None),
    )
    return jax.shard_map(shards, mesh=mesh, in_specs=in_specs, out_specs=out_specs, check_vma=False)
```

time: 497 us -> 484 us (0.974)
  local copies, waits for them, and re-layouts: 75.7 us -> 60.6 us
    convert_element_type x6 -> x1, local copies, waits for them, and re-layouts: 18.7 us -> 4.38 us  [shards(): arrived = exchange(dot('tkb,kbjg->jkgt', tok_parts, right_one).astype(bf))]
    optimization_barrier x0 -> x4, local copies, waits for them, and re-layouts: none -> 13.8 us  [the longest x1 4.41 us: shards(): d_sent, arrived = lax.optimization_barrier((d_sent, arrived))]
    all_to_all x5, local copies, waits for them, and re-layouts: 24.5 us -> 17.7 us  [exchange(): lax.all_to_all(value, 'tensor', split_axis=0, concat_axis=1, tiled=True)]
    transpose x4 -> x0, other arithmetic: 6.57 us -> none  [the longest x1 2.12 us: shards(): grad_right_two = jnp.transpose(reduced['right_two'], (1, 0, 2))]
    convert_element_type x0 -> x3, other arithmetic: none -> 6.44 us  [summed(): lax.psum_scatter(value, 'dp', scatter_dimension=0, tiled=False).astype(fp)]
    unnamed x29 -> x31, local copies, waits for them, and re-layouts: 21 us -> 16 us
    reshape x4 -> x6, local copies, waits for them, and re-layouts: 11.5 us -> 7.62 us  [the longest x5 6.83 us: summed(): value = value.reshape(lead, replicas, rows // replicas, width)]
    all_to_all x4 -> x5, starting transfers between devices: 19.7 us -> 23.4 us  [exchange(): lax.all_to_all(value, 'tensor', split_axis=0, concat_axis=1, tiled=True)]
  transfers between devices with their start and end apart: 8 -> 10, of which waited for: 5 -> 6; matrix products, arithmetic and copies ran while one was open for 16% -> 17% of each run, Pallas kernels for 0% -> 0%
where the time goes in v4:
time: 484 us; the launch traced here: 480 us
  waiting for transfers between devices  323 us (67%)
  local copies, waits for them, and re-layouts  60.6 us (13%)
  matrix products  50.1 us (10%)
  starting transfers between devices  24 us (5%)
  between operations  14 us (3%)
  other arithmetic  8.6 us (2%)
    all_to_all x5, waiting for transfers between devices, exchange(): lax.all_to_all(value, 'tensor', split_axis=0, concat_axis=1, tiled=True)  313 us
    dot_general x15, matrix products, dot(): return jnp.einsum(spec, left, right, preferred_element_type=fp)  50.1 us
    all_to_all x5, starting transfers between devices, exchange(): lax.all_to_all(value, 'tensor', split_axis=0, concat_axis=1, tiled=True)  23.4 us
    all_to_all x5, local copies, waits for them, and re-layouts, exchange(): lax.all_to_all(value, 'tensor', split_axis=0, concat_axis=1, tiled=True)  17.7 us
    unnamed x31, local copies, waits for them, and re-layouts  16 us
  transfers between devices with their start and end apart: 10, of which 6 were waited for; matrix products, arithmetic and copies ran while one was open for 17% of the time, Pallas kernels for 0%

profile of v4, /device:TPU:2, one launch (start us, length us, event | category | flops | bytes accessed | tf_op | source)
XLA Modules:
  0.0 480.5 jit_solution(12329406310412303749)
XLA Ops:
  12.8 4.4 copy.106
  17.2 6.0 %all-to-all-start = ((bf16[128,4,8,512]{3,2,1,0:T(8,128)(2,1)}), bf16[128,4,8,512]{3,2,1,0:T(8,128)(2,1)}, u32[]{:S(2)}, u32[]{:S(2)}) async-start(bf16[128,4,8,512]{3,2,1,0:T(8,128)(2,1)} %copy.106), calls=%async_computation | async-start | bytes 8388608 | tf_op jit(solution)/shard_map/all_to_all | solution.py:42
  24.0 4.9 %convert_bitcast_fusion.2 = bf16[128,4,8,512]{3,0,2,1:T(8,128)(2,1)} fusion(bf16[4,128,8,256]{3,2,1,0:T(8,128)(2,1)} %bitcast.195, bf16[512,4,256,1]{2,1,0,3:T(4,128)(2,1)S(1)} %bitcast.187), kind=kOutput, calls=%fused_computation.36 | convolution fusion | flops 1075838976 | bytes 7340032 | tf_op jit(solution)/shard_map/tkc,kjgc->jkgt/dot_general | solution.py:39
  28.9 87.6 %all-to-all-done = bf16[128,4,8,512]{3,2,1,0:T(8,128)(2,1)} async-done(((bf16[128,4,8,512]{3,2,1,0:T(8,128)(2,1)}), bf16[128,4,8,512]{3,2,1,0:T(8,128)(2,1)}, u32[]{:S(2)}, u32[]{:S(2)}) %all-to-all-start) | async-done | bytes 4194336 | tf_op jit(solution)/shard_map/all_to_all | solution.py:42
  116.4 4.9 %copy.107 = bf16[16,8,4,8,512]{4,3,2,1,0:T(8,128)(2,1)} copy(bf16[16,8,4,8,512]{4,3,2,0,1:T(8,128)(2,1)} %bitcast.8) | data formatting | bytes 8388608 | tf_op jit(solution)/shard_map/all_to_all | solution.py:42
  121.3 4.4 copy.112
  125.8 4.7 all-to-all-start.1
  130.5 4.1 copy.109
  134.6 6.2 %fusion.7 = (bf16[16,256,512]{1,2,0:T(8,128)(2,1)S(1)}, f32[16,512,256]{2,1,0:T(8,128)}) fusion(bf16[16,256,256]{2,1,0:T(8,128)(2,1)S(1)} %copy-done.6, bf16[16,32,8,512]{3,2,1,0:T(8,128)(2,1)} %bitcast.174), kind=kOutput, calls=%fused_computation.10 | convolution fusion | flops 1084227584 | bytes 18874368 | tf_op jit(solution)/shard_map/jbt,jbc->jct/dot_general | solution.py:39
  146.0 77.0 %all-to-all-done.1 = bf16[128,4,8,512]{3,2,1,0:T(8,128)(2,1)} async-done(((bf16[128,4,8,512]{3,2,1,0:T(8,128)(2,1)}), bf16[128,4,8,512]{3,2,1,0:T(8,128)(2,1)}, u32[]{:S(2)}, u32[]{:S(2)}) %all-to-all-start.1) | async-done | bytes 4194336 | tf_op jit(solution)/shard_map/all_to_all | solution.py:42
  223.0 4.9 %copy.113 = bf16[16,8,4,8,512]{4,3,2,1,0:T(8,128)(2,1)} copy(bf16[16,8,4,8,512]{4,3,2,0,1:T(8,128)(2,1)} %bitcast.16) | data formatting | bytes 8388608 | tf_op jit(solution)/shard_map/all_to_all | solution.py:42
  227.9 4.4 copy.117
  232.3 4.6 all-to-all-start.2
  236.9 7.9 %fusion.5 = bf16[16,256,512]{1,2,0:T(8,128)(2,1)S(1)} fusion(f32[16,512,256]{2,1,0:T(8,128)} %get-tuple-element.53, bf16[16,256,256]{2,1,0:T(8,128)(2,1)} %param.9, bf16[16,32,8,512]{3,2,1,0:T(8,128)(2,1)} %bitcast.172), kind=kOutput, calls=%fused_computation.6 | convolution fusion | flops 1094713344 | bytes 18874368 | tf_op jit(solution)/shard_map/jrt,jbr->jbt/dot_general | solution.py:39
  248.7 4.8 %multiply_convert_fusion.1 = bf16[16,256,256]{2,1,0:T(8,128)(2,1)S(1)} fusion(bf16[16,256,512]{1,2,0:T(8,128)(2,1)} %copy-done, bf16[16,32,8,512]{3,2,1,0:T(8,128)(2,1)} %bitcast.173), kind=kOutput, calls=%fused_computation.32 | convolution fusion | flops 1075838976 | bytes 10485760 | tf_op jit(solution)/shard_map/jbt,jrt->jbr/dot_general | solution.py:39
  259.3 70.0 %all-to-all-done.2 = bf16[32,16,8,512]{3,2,1,0:T(8,128)(2,1)} async-done(((bf16[32,16,8,512]{3,2,1,0:T(8,128)(2,1)}), bf16[32,16,8,512]{3,2,1,0:T(8,128)(2,1)}, u32[]{:S(2)}, u32[]{:S(2)}) %all-to-all-start.2) | async-done | bytes 4194336 | tf_op jit(solution)/shard_map/all_to_all | solution.py:42
  329.3 4.6 copy.118
  336.3 4.5 all-to-all-start.3
  345.9 4.0 convert_bitcast_fusion.3
  354.3 34.3 %all-to-all-done.3 = bf16[16,16,8,512]{3,2,1,0:T(8,128)(2,1)} async-done(((bf16[16,16,8,512]{3,2,1,0:T(8,128)(2,1)}), bf16[16,16,8,512]{3,2,1,0:T(8,128)(2,1)}, u32[]{:S(2)}, u32[]{:S(2)}) %all-to-all-start.3) | async-done | bytes 2097184 | tf_op jit(solution)/shard_map/all_to_all | solution.py:42
  394.3 3.6 all-to-all-start.4
  401.7 44.6 %all-to-all-done.4 = bf16[16,16,8,512]{3,2,1,0:T(8,128)(2,1)S(1)} async-done(((bf16[16,16,8,512]{3,2,1,0:T(8,128)(2,1)}), bf16[16,16,8,512]{3,2,1,0:T(8,128)(2,1)S(1)}, u32[]{:S(2)}, u32[]{:S(2)}) %all-to-all-start.4) | async-done | bytes 2097184 | tf_op jit(solution)/shard_map/all_to_all | solution.py:42
  449.0 3.5 fusion.51
  462.4 9.5 %reduce-scatter.12.cloned.1.call-done = bf16[1,2,64,1024]{3,2,1,0:T(8,128)(2,1)} async-done(((bf16[4,2,64,1024]{3,2,1,0:T(8,128)(2,1)}), bf16[1,2,64,1024]{3,2,1,0:T(8,128)(2,1)}) %reduce-scatter.12.cloned.1.call-update) | async-done | bytes 262160 | tf_op jit(solution)/shard_map/reduce_scatter | solution.py:49
  (69 shorter events, 57.2 us)
Async XLA Ops:
  17.2 6.0 %copy-start.11 = (bf16[512,1024]{1,0:T(8,128)(2,1)S(1)}, bf16[512,1024]{1,0:T(8,128)(2,1)}, u32[]{:S(2)}) copy-start(bf16[512,1024]{1,0:T(8,128)(2,1)} %param.11) | copy-start | bytes 3145732
  17.2 99.2 %all-to-all-start = ((bf16[128,4,8,512]{3,2,1,0:T(8,128)(2,1)}), bf16[128,4,8,512]{3,2,1,0:T(8,128)(2,1)}, u32[]{:S(2)}, u32[]{:S(2)}) async-start(bf16[128,4,8,512]{3,2,1,0:T(8,128)(2,1)} %copy.106), calls=%async_computation | async-start | bytes 8388608 | tf_op jit(solution)/shard_map/all_to_all | solution.py:42
  116.4 4.9 %copy-start.3 = (bf16[128,4,8,512]{3,0,2,1:T(8,128)(2,1)S(1)}, bf16[128,4,8,512]{3,0,2,1:T(8,128)(2,1)}, u32[]{:S(2)}) copy-start(bf16[128,4,8,512]{3,0,2,1:T(8,128)(2,1)} %convert_bitcast_fusion.2) | copy-start | bytes 12582916
  125.8 97.2 %all-to-all-start.1 = ((bf16[128,4,8,512]{3,2,1,0:T(8,128)(2,1)}), bf16[128,4,8,512]{3,2,1,0:T(8,128)(2,1)}, u32[]{:S(2)}, u32[]{:S(2)}) async-start(bf16[128,4,8,512]{3,2,1,0:T(8,128)(2,1)} %copy.112), calls=%async_computation.1 | async-start | bytes 8388608 | tf_op jit(solution)/shard_map/all_to_all | solution.py:42
  130.5 4.1 copy-start.6
  134.6 8.1 %copy-start.7 = (bf16[16,256,256]{1,2,0:T(8,128)(2,1)S(1)}, bf16[16,256,256]{1,2,0:T(8,128)(2,1)}, u32[]{:S(2)}) copy-start(bf16[16,256,256]{1,2,0:T(8,128)(2,1)} %copy.109) | copy-start | bytes 6291460
  140.8 1.9 copy-start
  223.0 4.9 %copy-start.4 = (bf16[32,16,8,512]{3,0,2,1:T(8,128)(2,1)S(1)}, bf16[32,16,8,512]{3,0,2,1:T(8,128)(2,1)}, u32[]{:S(2)}) copy-start(bf16[32,16,8,512]{3,0,2,1:T(8,128)(2,1)} %convert_bitcast_fusion) | copy-start | bytes 12582916
  232.3 97.0 %all-to-all-start.2 = ((bf16[32,16,8,512]{3,2,1,0:T(8,128)(2,1)}), bf16[32,16,8,512]{3,2,1,0:T(8,128)(2,1)}, u32[]{:S(2)}, u32[]{:S(2)}) async-start(bf16[32,16,8,512]{3,2,1,0:T(8,128)(2,1)} %copy.117), calls=%async_computation.2 | async-start | bytes 8388608 | tf_op jit(solution)/shard_map/all_to_all | solution.py:42
  236.8 113.1 %reduce-scatter.6.cloned.1.call-start = ((), (), s32[]{:S(2)}) async-start(), calls=%async_computation.10 | async-start | bytes 2621440 | tf_op jit(solution)/shard_map/reduce_scatter | solution.py:49
  236.9 7.9 %copy-start.5 = (bf16[16,8,4,8,512]{4,3,2,1,0:T(8,128)(2,1)S(1)}, bf16[16,8,4,8,512]{4,3,2,1,0:T(8,128)(2,1)}, u32[]{:S(2)}) copy-start(bf16[16,8,4,8,512]{4,3,2,1,0:T(8,128)(2,1)} %copy.107) | copy-start | bytes 12582916
  244.8 2.0 copy-start.1
  248.4 103.7 %reduce-scatter.8.cloned.1.call-start = ((), (), s32[]{:S(2)}) async-start(), calls=%async_computation.11 | async-start | bytes 2621440 | tf_op jit(solution)/shard_map/reduce_scatter | solution.py:49
  255.0 2.8 copy-start.2
  336.3 4.5 copy-start.12
  336.3 52.3 %all-to-all-start.3 = ((bf16[16,16,8,512]{3,2,1,0:T(8,128)(2,1)}), bf16[16,16,8,512]{3,2,1,0:T(8,128)(2,1)}, u32[]{:S(2)}, u32[]{:S(2)}) async-start(bf16[16,16,8,512]{3,2,1,0:T(8,128)(2,1)} %copy.122), calls=%async_computation.3 | async-start | bytes 4194304 | tf_op jit(solution)/shard_map/all_to_all | solution.py:42
  340.8 115.7 %reduce-scatter.14.cloned.1.call-start = ((), (), s32[]{:S(2)}) async-start(), calls=%async_computation.14 | async-start | bytes 2621440 | tf_op jit(solution)/shard_map/reduce_scatter | solution.py:49
  394.3 52.0 %all-to-all-start.4 = ((bf16[16,16,8,512]{3,2,1,0:T(8,128)(2,1)}), bf16[16,16,8,512]{3,2,1,0:T(8,128)(2,1)S(1)}, u32[]{:S(2)}, u32[]{:S(2)}) async-start(bf16[16,16,8,512]{3,2,1,0:T(8,128)(2,1)} %copy.128), calls=%async_computation.6 | async-start | bytes 4194304 | tf_op jit(solution)/shard_map/all_to_all | solution.py:42
  397.9 64.5 %reduce-scatter.10.cloned.1.call-start = ((), (), s32[]{:S(2)}) async-start(), calls=%async_computation.12 | async-start | bytes 1310720 | tf_op jit(solution)/shard_map/reduce_scatter | solution.py:49
  401.4 70.5 %reduce-scatter.12.cloned.1.call-start = ((), (), s32[]{:S(2)}) async-start(), calls=%async_computation.13 | async-start | bytes 1310720 | tf_op jit(solution)/shard_map/reduce_scatter | solution.py:49
  446.5 1.4 copy-start.10
  446.5 2.5 copy-start.8
  452.5 6.2 %copy-start.9 = (bf16[4,256,1024]{2,1,0:T(8,128)(2,1)S(1)}, bf16[4,256,1024]{2,1,0:T(8,128)(2,1)}, u32[]{:S(2)}) copy-start(bf16[4,256,1024]{2,1,0:T(8,128)(2,1)} %param.7) | copy-start | bytes 6291460
Sparse Core Ops, SparseCore 0:
  248.6 31.4 reduce-scatter.5
  282.8 31.4 reduce-scatter.7
  346.1 31.5 reduce-scatter.13
  401.6 25.0 reduce-scatter.9
  449.1 22.7 reduce-scatter.11
